TPU v7x, 256 devices: a whole 4x4x8 slice. The times are simulated.
256 devices in a mesh: owner: 8 (over x, core), dp: 32 (over z, y).
Axes of the slice: x: 4, y: 4, z: 8, core: 2. Of those that a mesh axis runs over, the one named last changes fastest.
Arguments:
- documents: bfloat16 [262144, 768], P(('owner', 'dp')), may hold values from -6 to 6
- enc_weight: bfloat16 [768, 768], replicated, may hold values from -0.21875 to 0.21875
- label_slab: bfloat16 [4096, 768], P('owner'), may hold values from -0.21875 to 0.21875
- row_scale: bfloat16 [4096], P('owner'), may hold values from 0.25 to 4
- shortlist: int32 [262144, 32], P(('owner', 'dp')), may hold values from 0 to 1023, as said below
- positive: int32 [262144, 32], P(('owner', 'dp')), may hold values 0 or 1
- request_ids: int32 [2048, 128], P(('owner', 'dp')), may hold values from 0 to 511
- counts: int32 [256, 8], P(('owner', 'dp')), may hold values from 16 to 128, as said below
Outputs:
- slab_grad: float32 [4096, 768], P(('owner', 'dp'))
- enc_grad: float32 [768, 768], replicated
Inputs may be any that keep to these rules, and one draw needn't show every extreme that they name: shortlist[n, k] = p * 128 + j names slot j of owner p among the requests of the device holding document n, with j below that device's count for owner p. `counts`: for each index of dp one owner receives 128 live slots from every device of that index. `request_ids`: slots at or past a count are never named by a shortlist.
All inputs are finite; a program needn't handle non-finite values. No bound on the sum of `positive` on one device may be relied on, other than what follows from the above.
Results may differ from a plain program's by a relative error of at most 0.0018.
Values may be sent and summed in bfloat16 or wider, within the bound.
A program may use at most 64 MiB of HBM per device.

v0:
```python
import jax
import jax.numpy as jnp
from jax import lax
from jax.sharding import PartitionSpec as P


def body(documents, enc_weight, label_slab, row_scale, shortlist, positive, request_ids, counts):
    owners = lax.axis_size("owner")
    capacity = request_ids.shape[1]
    feature_width = documents.shape[1]
    slot_count = owners * capacity
    pre_act = jnp.dot(documents, enc_weight, preferred_element_type=jnp.float32)
    squashed = jnp.tanh(pre_act)
    embedded = (documents.astype(jnp.float32) + squashed).astype(jnp.bfloat16)
    served = lax.all_to_all(request_ids, "owner", split_axis=0, concat_axis=0, tiled=True)
    flat_ids = served.reshape(-1)
    picked = label_slab[flat_ids].reshape(owners, capacity, feature_width)
    picked_scale = row_scale[flat_ids].reshape(owners, capacity)
    fetched, fetched_scale = (
        lax.all_to_all(picked, "owner", split_axis=0, concat_axis=0, tiled=True),
        lax.all_to_all(picked_scale, "owner", split_axis=0, concat_axis=0, tiled=True),
    )
    fetched = fetched.reshape(slot_count, feature_width)
    scale_row = fetched_scale.reshape(slot_count).astype(jnp.float32)
    scores = lax.dot_general(
        embedded, fetched, (((1,), (1,)), ((), ())), preferred_element_type=jnp.float32
    )
    logits = scores * scale_row[None, :]
    chance = jax.nn.sigmoid(logits)
    usable = (
        (jnp.arange(capacity, dtype=jnp.int32)[None, :] < counts[0][:, None])
        .reshape(slot_count)
        .astype(jnp.float32)
    )
    slot_iota = jnp.arange(slot_count, dtype=jnp.int32)
    matches = shortlist[:, :, None] == slot_iota[None, None, :]
    hit_count = jnp.sum(matches, axis=1, dtype=jnp.float32)
    labels_on = jnp.sum(jnp.where(matches, positive[:, :, None].astype(jnp.float32), 0.0), axis=1)
    dlogit = ((hit_count + usable[None, :]) * chance - labels_on) / shortlist.shape[1]
    dscore = (dlogit * scale_row[None, :]).astype(jnp.bfloat16)
    slot_grads = lax.dot_general(
        dscore, embedded, (((0,), (0,)), ((), ())), preferred_element_type=jnp.float32
    )
    slot_grads = slot_grads.astype(jnp.bfloat16).reshape(owners, capacity, feature_width)
    returned = lax.all_to_all(slot_grads, "owner", split_axis=0, concat_axis=0, tiled=True)
    owner_sum = jnp.zeros((label_slab.shape[0], feature_width), jnp.float32)
    owner_sum = owner_sum.at[flat_ids].add(
        returned.reshape(slot_count, feature_width).astype(jnp.float32)
    )
    slab_grad = lax.psum_scatter(owner_sum, "dp", scatter_dimension=0, tiled=True)
    emb_grad = jnp.dot(dscore, fetched, preferred_element_type=jnp.float32)
    inner_grad = (emb_grad * (1.0 - squashed * squashed)).astype(jnp.bfloat16)
    enc_local = lax.dot_general(
        documents, inner_grad, (((0,), (0,)), ((), ())), preferred_element_type=jnp.float32
    )
    enc_grad = lax.psum(enc_local, ("owner", "dp"))
    return (slab_grad, enc_grad)


def solution(mesh):
    return jax.shard_map(
        body,
        mesh=mesh,
        in_specs=(
            P(("owner", "dp"), None),
            P(),
            P("owner", None),
            P("owner"),
            P(("owner", "dp"), None),
            P(("owner", "dp"), None),
            P(("owner", "dp"), None),
            P(("owner", "dp"), None),
        ),
        out_specs=(P(("owner", "dp"), None), P()),
        check_vma=False,
    )
```

profile of v0, /device:TPU:1, one launch (start us, length us, event | category | flops | bytes accessed | tf_op | source)
XLA Modules:
  0.0 392.8 jit_solution(16053684413078447775)
XLA Ops:
  8.0 0.0 copy-start
  8.0 0.0 copy-start.2
  8.0 11.1 %all_to_all.28 = s32[8,1,128]{2,1,0:T(1,128)S(1)} all-to-all(s32[8,1,128]{2,1,0:T(1,128)} %bitcast.30), channel_id=1, replica_groups=mesh['owner'=8,'dp'=32] {'owner'}, dimensions={0} | all-to-all | bytes 8192 | tf_op jit(solution)/shard_map/all_to_all | solution.py:15
  19.1 6.2 %gather_fusion.1 = bf16[1024]{0:T(1024)(128)(2,1)S(1)} fusion(bf16[512]{0:T(512)(128)(2,1)} %param.11, s32[1024]{0:T(1024)S(1)} %broadcast_clamp_fusion), kind=kCustom, calls=%fused_computation.1 | custom fusion | bytes 8192 | tf_op jit(solution)/shard_map/gather | solution.py:18
  25.4 0.6 copy.21
  26.0 3.9 all-to-all-start.2
  29.9 0.9 convert_element_type.59
  30.8 0.2 copy.22
  31.0 0.0 copy-done.2
  31.0 0.2 copy.20
  31.2 0.0 copy-done.1
  31.2 5.2 %gather_fusion = bf16[1024,768]{1,0:T(8,128)(2,1)} fusion(bf16[512,768]{1,0:T(8,128)(2,1)S(1)} %copy-done.1, s32[1024]{0:T(1024)S(1)} %broadcast_clamp_fusion), kind=kCustom, calls=%fused_computation | custom fusion | bytes 3149824 | tf_op jit(solution)/shard_map/gather | solution.py:17
  36.5 0.0 all-to-all-done.2
  36.5 4.8 %all-to-all-start.1 = ((bf16[8,128,768]{2,1,0:T(8,128)(2,1)}), bf16[8,128,768]{2,1,0:T(8,128)(2,1)}, u32[]{:S(2)}, u32[]{:S(2)}) async-start(bf16[8,128,768]{2,1,0:T(8,128)(2,1)} %bitcast.5), calls=%async_computation.1 | async-start | bytes 3145728 | tf_op jit(solution)/shard_map/all_to_all | solution.py:20
  41.3 47.7 %convert_reduce_fusion = (f32[1024,1024]{1,0:T(8,128)}, f32[1024,1024]{1,0:T(8,128)}) fusion(s32[1024,32]{1,0:T(8,128)S(1)} %copy.20, f32[1024,32]{1,0:T(8,128)S(1)} %copy.22), kind=kLoop, calls=%fused_computation.4 | loop fusion | flops 199229440 | bytes 8650752 | tf_op jit(solution)/shard_map/reduce_sum | solution.py:37
  89.0 0.0 copy-done.3
  89.0 0.1 convert_bitcast_fusion
  89.1 4.6 %fusion.4 = f32[1024,768]{1,0:T(8,128)} fusion(bf16[1024,768]{1,0:T(8,128)(2,1)} %param.8, bf16[768,768]{1,0:T(8,128)(2,1)S(1)} %copy-done), kind=kOutput, calls=%fused_computation.20 | convolution fusion | flops 1207959552 | bytes 5898240 | tf_op jit(solution)/shard_map/dot_general | solution.py:12
  93.8 0.0 all-to-all-done.1
  93.8 7.5 %multiply_convert_fusion = bf16[1024,1024]{1,0:T(8,128)(2,1)S(1)} fusion(f32[1024,1024]{1,0:T(8,128)} %get-tuple-element.11, f32[1024,1024]{1,0:T(8,128)} %get-tuple-element.10, bf16[1024,768]{1,0:T(8,128)(2,1)} %bitcast.6, f32[1024]{0:T(1024)S(1)} %broadcast_multiply_fusion, f32[1024]{0:T(1024)S(1)} %bitcast.28, f32[1024]{0:T(1024)S(1)} %convert_bitcast_fusion, ...), kind=kOutput, calls=%fused_computation.6 | convolution fusion | flops 1622409216 | bytes 16789504 | tf_op jit(solution)/shard_map/dot_general | solution.py:25
  101.3 3.1 convolution_convert_fusion
  104.5 0.0 copy-done.6
  104.5 4.8 %all-to-all-start.3 = ((bf16[8,128,768]{2,1,0:T(8,128)(2,1)}), bf16[8,128,768]{2,1,0:T(8,128)(2,1)S(1)}, u32[]{:S(2)}, u32[]{:S(2)}) async-start(bf16[8,128,768]{2,1,0:T(8,128)(2,1)} %bitcast.24), calls=%async_computation.3 | async-start | bytes 3145728 | tf_op jit(solution)/shard_map/all_to_all | solution.py:45
  109.3 0.0 all-reduce.2.cloned.1.call-start
  109.3 10.1 %convolution_bitcast_fusion = f32[768,768]{0,1:T(8,128)} fusion(bf16[1024,768]{1,0:T(8,128)(2,1)} %param.8, f32[1024,768]{1,0:T(8,128)} %fusion.4, bf16[1024,1024]{1,0:T(8,128)(2,1)} %copy-done.6, bf16[1024,768]{1,0:T(8,128)(2,1)} %bitcast.6), kind=kOutput, calls=%fused_computation.11 | convolution fusion | flops 2821718016 | bytes 10747904 | tf_op jit(solution)/shard_map/dot_general | solution.py:53
  119.4 0.0 all-reduce.2.cloned.1.call-update
  119.4 0.0 reduce-scatter.2.cloned.1.call-start
  119.5 10.6 %all-to-all-done.3 = bf16[8,128,768]{2,1,0:T(8,128)(2,1)S(1)} async-done(((bf16[8,128,768]{2,1,0:T(8,128)(2,1)}), bf16[8,128,768]{2,1,0:T(8,128)(2,1)S(1)}, u32[]{:S(2)}, u32[]{:S(2)}) %all-to-all-start.3) | async-done | bytes 1572896 | tf_op jit(solution)/shard_map/all_to_all | solution.py:45
  130.0 8.5 %scatter_custom_fusion = f32[512,768]{1,0:T(8,128)} fusion(s32[1024]{0:T(1024)S(1)} %bitcast.26, bf16[1024,768]{1,0:T(8,128)(2,1)S(1)} %bitcast.23, f32[]{:T(128)} %constant.5.clone.1), kind=kCustom, calls=%fused_computation.7 | custom fusion | flops 1572864 | bytes 3145732 | tf_op jit(solution)/shard_map/scatter-add | solution.py:47
  138.5 0.0 reduce-scatter.2.cloned.1.call-update
  138.5 243.7 %all-reduce.2.cloned.1.call-done = f32[768,768]{0,1:T(8,128)} async-done(((f32[768,768]{0,1:T(8,128)}), f32[768,768]{0,1:T(8,128)}) %all-reduce.2.cloned.1.call-update) | async-done | bytes 2359312 | tf_op jit(solution)/shard_map/psum | solution.py:56
  382.3 3.0 copy.23
  (13 shorter events, 0.0 us)
Async XLA Ops:
  8.0 81.1 %copy-start = (bf16[768,768]{1,0:T(8,128)(2,1)S(1)}, bf16[768,768]{1,0:T(8,128)(2,1)}, u32[]{:S(2)}) copy-start(bf16[768,768]{1,0:T(8,128)(2,1)} %param.9) | copy-start | bytes 3538948
  8.0 23.0 %copy-start.2 = (s32[1024,32]{0,1:T(8,128)S(1)}, s32[1024,32]{0,1:T(8,128)}, u32[]{:S(2)}) copy-start(s32[1024,32]{0,1:T(8,128)} %param.12) | copy-start | bytes 393220
  8.0 23.2 %copy-start.1 = (bf16[512,768]{1,0:T(8,128)(2,1)S(1)}, bf16[512,768]{1,0:T(8,128)(2,1)}, u32[]{:S(2)}) copy-start(bf16[512,768]{1,0:T(8,128)(2,1)} %param.10) | copy-start | bytes 2359300
  26.0 10.5 %all-to-all-start.2 = ((bf16[8,1,128]{2,1,0:T(2,128)(2,1)}), bf16[8,1,128]{2,1,0:T(2,128)(2,1)S(1)}, u32[]{:S(2)}, u32[]{:S(2)}) async-start(bf16[8,1,128]{2,1,0:T(2,128)(2,1)} %copy.21), calls=%async_computation.2 | async-start | bytes 8192 | tf_op jit(solution)/shard_map/all_to_all | solution.py:21
  36.5 57.3 %all-to-all-start.1 = ((bf16[8,128,768]{2,1,0:T(8,128)(2,1)}), bf16[8,128,768]{2,1,0:T(8,128)(2,1)}, u32[]{:S(2)}, u32[]{:S(2)}) async-start(bf16[8,128,768]{2,1,0:T(8,128)(2,1)} %bitcast.5), calls=%async_computation.1 | async-start | bytes 3145728 | tf_op jit(solution)/shard_map/all_to_all | solution.py:20
  41.3 47.8 %copy-start.3 = (s32[1,8]{1,0:T(1,128)S(1)}, s32[1,8]{1,0:T(1,128)}, u32[]{:S(2)}) copy-start(s32[1,8]{1,0:T(1,128)} %param.15) | copy-start | bytes 100
  89.1 4.7 %copy-start.4 = (bf16[1024,768]{1,0:T(8,128)(2,1)S(1)}, bf16[1024,768]{1,0:T(8,128)(2,1)}, u32[]{:S(2)}) copy-start(bf16[1024,768]{1,0:T(8,128)(2,1)} %param.8) | copy-start | bytes 4718596
  93.8 7.6 %copy-start.5 = (f32[1024,768]{1,0:T(8,128)S(1)}, f32[1024,768]{1,0:T(8,128)}, u32[]{:S(2)}) copy-start(f32[1024,768]{1,0:T(8,128)} %fusion.4) | copy-start | bytes 9437188
  101.3 3.2 copy-start.6
  104.5 25.5 %all-to-all-start.3 = ((bf16[8,128,768]{2,1,0:T(8,128)(2,1)}), bf16[8,128,768]{2,1,0:T(8,128)(2,1)S(1)}, u32[]{:S(2)}, u32[]{:S(2)}) async-start(bf16[8,128,768]{2,1,0:T(8,128)(2,1)} %bitcast.24), calls=%async_computation.3 | async-start | bytes 3145728 | tf_op jit(solution)/shard_map/all_to_all | solution.py:45
  109.3 273.0 %all-reduce.2.cloned.1.call-start = ((), (), s32[]{:S(2)}) async-start(), calls=%async_computation.6 | async-start | bytes 4718592 | tf_op jit(solution)/shard_map/psum | solution.py:56
  119.4 265.9 %reduce-scatter.2.cloned.1.call-start = ((), (), s32[]{:S(2)}) async-start(), calls=%async_computation.5 | async-start | bytes 1622016 | tf_op jit(solution)/shard_map/reduce_scatter | solution.py:50
Sparse Core Ops, SparseCore 0:
  119.5 262.6 all-reduce.1
Sparse Core Ops, SparseCore 1:
  138.6 212.9 reduce-scatter.1
where the time goes:
time: 394 us; the launch traced here: 393 us
  waiting for transfers between devices  254 us (64%)
  other arithmetic  57.3 us (15%)
  matrix products  25.4 us (6%)
  between operations  15.6 us (4%)
  local copies, waits for them, and re-layouts  15.5 us (4%)
  starting transfers between devices  13.6 us (3%)
  blocking collectives  11.1 us (3%)
    psum x1, waiting for transfers between devices, body(): enc_grad = lax.psum(enc_local, ('owner', 'dp'))  244 us
    reduce_sum x1, other arithmetic, body(): hit_count = jnp.sum(matches, axis=1, dtype=jnp.float32)  47.7 us
    all_to_all x1, blocking collectives, body(): lax.all_to_all(request_ids, 'owner', split_axis=0, concat_axis=0, tiled=T...  11.1 us
    all_to_all x1, waiting for transfers between devices, body(): lax.all_to_all(slot_grads, 'owner', split_axis=0, concat_axis=0, tiled=True)  10.6 us
    dot_general x1, matrix products, body(): lax.dot_general(documents, inner_grad, (((0,), (0,)), ((), ())), preferre...  10.1 us
    scatter-add x1, other arithmetic, body(): owner_sum.at[flat_ids]  8.51 us
  transfers between devices with their start and end apart: 5, of which 2 were waited for; matrix products, arithmetic and copies ran while one was open for 21% of the time, Pallas kernels for 0%

commit v1 on v0

--- a/solution.py
+++ b/solution.py
@@ -1,10 +1,253 @@
+import functools
+
 import jax
 import jax.numpy as jnp
 from jax import lax
+from jax.experimental import pallas as pl
+from jax.experimental.pallas import tpu as pltpu
 from jax.sharding import PartitionSpec as P
 
-
-def body(documents, enc_weight, label_slab, row_scale, shortlist, positive, request_ids, counts):
+MESH = pl.DeviceIdType.MESH
+F32 = jnp.float32
+BF16 = jnp.bfloat16
+
+
+def torus(mesh):
+    owners, groups = mesh.shape["owner"], mesh.shape["dp"]
+    nx = owners // 2
+    ny = 4 if groups >= 16 else 2
+    return nx, ny, groups // ny
+
+
+def place(ny):
+    o, d = lax.axis_index("owner"), lax.axis_index("dp")
+    return o // 2, d % ny, d // ny, o % 2
+
+
+def device(ny, x, y, z, c):
+    return {"owner": x * 2 + c, "dp": z * ny + y}
+
+
+def remote(src, dst, send, recv, target):
+    return pltpu.make_async_remote_copy(
+        src_ref=src, dst_ref=dst, send_sem=send, recv_sem=recv, device_id=target, device_id_type=MESH
+    )
+
+
+def tail_kernel(dims, own, enc, slab_out, enc_out, sib, accp, accq, gotp, gotq, allp, allq, gota, gotb, acca, accb,
+                gota2, gotb2, s_sib, r_sib, s_p, r_p, s_q, r_q, s_p2, r_p2, s_q2, r_q2, s_p3, r_p3, s_q3, r_q3,
+                s_a, r_a, s_b, r_b, s_a2, r_a2, s_b2, r_b2, s_end, r_end):
+    nx, ny, nz = dims
+    x, y, z, c = place(ny)
+    plane = [(i, j) for i in range(nx) for j in range(ny) if (i, j) != (0, 0)]
+    rings = list(range(1, nz))
+    cols = list(range(1, ny))
+    here = x * ny + y
+    rows_p, rows_q = accp.shape[1], accq.shape[1]
+    wide = accp.shape[2]
+
+    def at_plane(i, j):
+        return lax.rem(x + i, nx), lax.rem(y + j, ny)
+
+    bar = pltpu.get_barrier_semaphore()
+    for i, j in plane:
+        px, py = at_plane(i, j)
+        pl.semaphore_signal(bar, inc=1, device_id=device(ny, px, py, z, c), device_id_type=MESH)
+    for k in rings:
+        pl.semaphore_signal(bar, inc=1, device_id=device(ny, x, y, lax.rem(z + k, nz), c), device_id_type=MESH)
+    pl.semaphore_signal(bar, inc=1, device_id=device(ny, x, y, z, 1 - c), device_id_type=MESH)
+    pl.semaphore_wait(bar, len(plane) + len(rings) + 1)
+
+    swap = remote(enc.at[1 - c], sib, s_sib, r_sib, device(ny, x, y, z, 1 - c))
+    swap.start()
+    first_a, first_b = [], []
+    for j in cols:
+        py = lax.rem(y + j, ny)
+        first_a.append(remote(own.at[:, py, :, 0:wide], gota.at[j - 1], s_a.at[j - 1], r_a.at[j - 1],
+                              device(ny, x, py, z, c)))
+    for k in rings:
+        pz = lax.rem(z + k, nz)
+        first_b.append(remote(own.at[pz, :, :, wide:], gotb.at[k - 1], s_b.at[k - 1], r_b.at[k - 1],
+                              device(ny, x, y, pz, c)))
+    for copy in first_a + first_b:
+        copy.start()
+    swap.wait()
+
+    def join_p(q, _):
+        rows = pl.ds(pl.multiple_of(q * rows_p, 8), rows_p)
+        accp[q] = enc[c, rows, 0:wide] + sib[rows, 0:wide]
+        return 0
+
+    def join_q(q, _):
+        rows = pl.ds(pl.multiple_of(q * rows_q, 8), rows_q)
+        accq[q] = enc[c, rows, wide:] + sib[rows, wide:]
+        return 0
+
+    lax.fori_loop(0, nx * ny, join_p, 0)
+    lax.fori_loop(0, nz, join_q, 0)
+    p1, q1 = [], []
+    for n, (i, j) in enumerate(plane):
+        px, py = at_plane(i, j)
+        p1.append(remote(accp.at[px * ny + py], gotp.at[n], s_p.at[n], r_p.at[n], device(ny, px, py, z, c)))
+    for k in rings:
+        pz = lax.rem(z + k, nz)
+        q1.append(remote(accq.at[pz], gotq.at[k - 1], s_q.at[k - 1], r_q.at[k - 1], device(ny, x, y, pz, c)))
+    for copy in p1 + q1:
+        copy.start()
+
+    for copy in first_a:
+        copy.wait()
+
+    def join_a(q, _):
+        total = own[q, y, :, 0:wide]
+        for j in cols:
+            total += gota[j - 1, q]
+        acca[q] = total
+        return 0
+
+    lax.fori_loop(0, nz, join_a, 0)
+    second_a, second_b = [], []
+    for k in rings:
+        pz = lax.rem(z + k, nz)
+        second_a.append(remote(acca.at[pz], gota2.at[k - 1], s_a2.at[k - 1], r_a2.at[k - 1], device(ny, x, y, pz, c)))
+    for copy in second_a:
+        copy.start()
+    for copy in first_b:
+        copy.wait()
+
+    def join_b(q, _):
+        total = own[z, q, :, wide:]
+        for k in rings:
+            total += gotb[k - 1, q]
+        accb[q] = total
+        return 0
+
+    lax.fori_loop(0, ny, join_b, 0)
+    for j in cols:
+        py = lax.rem(y + j, ny)
+        second_b.append(remote(accb.at[py], gotb2.at[j - 1], s_b2.at[j - 1], r_b2.at[j - 1],
+                               device(ny, x, py, z, c)))
+    for copy in second_b:
+        copy.start()
+
+    for copy in p1:
+        copy.wait()
+    total = accp[here]
+    for n in range(len(plane)):
+        total += gotp[n]
+    allp[z] = total
+    p2, q2 = [], []
+    for k in rings:
+        pz = lax.rem(z + k, nz)
+        p2.append(remote(allp.at[z], allp.at[z], s_p2.at[k - 1], r_p2.at[k - 1], device(ny, x, y, pz, c)))
+    for copy in p2:
+        copy.start()
+    for copy in q1:
+        copy.wait()
+    total = accq[z]
+    for k in rings:
+        total += gotq[k - 1]
+    allq[here] = total
+    for n, (i, j) in enumerate(plane):
+        px, py = at_plane(i, j)
+        q2.append(remote(allq.at[here], allq.at[here], s_q2.at[n], r_q2.at[n], device(ny, px, py, z, c)))
+    for copy in q2:
+        copy.start()
+
+    for copy in second_a:
+        copy.wait()
+    total = acca[z]
+    for k in rings:
+        total += gota2[k - 1]
+    slab_out[:, 0:wide] = total
+    for copy in second_b:
+        copy.wait()
+    total = accb[y]
+    for j in cols:
+        total += gotb2[j - 1]
+    slab_out[:, wide:] = total
+
+    p3, q3 = [], []
+    for copy in p2:
+        copy.wait()
+    total = allp[0]
+    for k in range(1, nz):
+        total += allp[k]
+    rows = pl.ds(pl.multiple_of(here * rows_p, 8), rows_p)
+    enc_out[c, rows, 0:wide] = total
+    for n, (i, j) in enumerate(plane):
+        px, py = at_plane(i, j)
+        part = enc_out.at[c, rows, 0:wide]
+        p3.append(remote(part, part, s_p3.at[n], r_p3.at[n], device(ny, px, py, z, c)))
+    for copy in p3:
+        copy.start()
+    for copy in q2:
+        copy.wait()
+    total = allq[0]
+    for k in range(1, nx * ny):
+        total += allq[k]
+    rows = pl.ds(pl.multiple_of(z * rows_q, 8), rows_q)
+    enc_out[c, rows, wide:] = total
+    for k in rings:
+        pz = lax.rem(z + k, nz)
+        part = enc_out.at[c, rows, wide:]
+        q3.append(remote(part, part, s_q3.at[k - 1], r_q3.at[k - 1], device(ny, x, y, pz, c)))
+    for copy in q3:
+        copy.start()
+    for copy in p3 + q3:
+        copy.wait()
+    last = remote(enc_out.at[c], enc_out.at[c], s_end, r_end, device(ny, x, y, z, 1 - c))
+    last.start()
+    last.wait()
+
+
+def tail(dims, own, enc):
+    nx, ny, nz = dims
+    half, width = enc.shape[1:]
+    depth = own.shape[2]
+    plane = nx * ny
+    wide = 2 * width // 3
+    slim = width - wide
+    vm = lambda *shape: pltpu.VMEM(shape, F32)
+    dma = lambda n: [pltpu.SemaphoreType.DMA((n,))] * 2
+    return pl.pallas_call(
+        functools.partial(tail_kernel, dims),
+        out_shape=(jax.ShapeDtypeStruct((depth, width), F32), jax.ShapeDtypeStruct((2, half, width), F32)),
+        in_specs=[pl.BlockSpec(memory_space=pltpu.VMEM)] * 2,
+        out_specs=[pl.BlockSpec(memory_space=pltpu.VMEM)] * 2,
+        scratch_shapes=[
+            vm(half, width),
+            vm(plane, half // plane, wide),
+            vm(nz, half // nz, slim),
+            vm(plane - 1, half // plane, wide),
+            vm(nz - 1, half // nz, slim),
+            vm(nz, half // plane, wide),
+            vm(plane, half // nz, slim),
+            vm(ny - 1, nz, depth, wide),
+            vm(nz - 1, ny, depth, slim),
+            vm(nz, depth, wide),
+            vm(ny, depth, slim),
+            vm(nz - 1, depth, wide),
+            vm(ny - 1, depth, slim),
+            pltpu.SemaphoreType.DMA,
+            pltpu.SemaphoreType.DMA,
+            *dma(plane - 1), *dma(nz - 1),
+            *dma(nz - 1), *dma(plane - 1),
+            *dma(plane - 1), *dma(nz - 1),
+            *dma(ny - 1), *dma(nz - 1),
+            *dma(nz - 1), *dma(ny - 1),
+            pltpu.SemaphoreType.DMA,
+            pltpu.SemaphoreType.DMA,
+        ],
+        compiler_params=pltpu.CompilerParams(
+            collective_id=1, has_side_effects=True, vmem_limit_bytes=48 * 2**20
+        ),
+        cost_estimate=pl.CostEstimate(flops=10**8, bytes_accessed=10**7, transcendentals=0),
+        name="reduce_gradients",
+    )(own, enc)
+
+
+def body(dims, documents, enc_weight, label_slab, row_scale, shortlist, positive, request_ids, counts):
     owners = lax.axis_size("owner")
     capacity = request_ids.shape[1]
     feature_width = documents.shape[1]
@@ -47,19 +290,24 @@
     owner_sum = owner_sum.at[flat_ids].add(
         returned.reshape(slot_count, feature_width).astype(jnp.float32)
     )
-    slab_grad = lax.psum_scatter(owner_sum, "dp", scatter_dimension=0, tiled=True)
     emb_grad = jnp.dot(dscore, fetched, preferred_element_type=jnp.float32)
     inner_grad = (emb_grad * (1.0 - squashed * squashed)).astype(jnp.bfloat16)
     enc_local = lax.dot_general(
         documents, inner_grad, (((0,), (0,)), ((), ())), preferred_element_type=jnp.float32
     )
-    enc_grad = lax.psum(enc_local, ("owner", "dp"))
+    nx, ny, nz = dims
+    slab_grad, enc_grad = tail(
+        dims,
+        owner_sum.reshape(nz, ny, owner_sum.shape[0] // (nz * ny), feature_width),
+        enc_local.reshape(2, feature_width // 2, feature_width),
+    )
+    enc_grad = enc_grad.reshape(feature_width, feature_width)
     return (slab_grad, enc_grad)
 
 
 def solution(mesh):
     return jax.shard_map(
-        body,
+        functools.partial(body, torus(mesh)),
         mesh=mesh,
         in_specs=(
             P(("owner", "dp"), None),

time: 394 us -> 196 us (0.50)
  waiting for transfers between devices: 254 us -> 11 us
  Pallas kernels: 0 us -> 61.7 us
  between operations: 15.6 us -> 0.76 us
    psum x1 -> x0, waiting for transfers between devices: 244 us -> none  [body(): enc_grad = lax.psum(enc_local, ('owner', 'dp'))]
    pallas_call x0 -> x1, Pallas kernels: none -> 61.7 us  [tail(): pl.pallas_call(functools.partial(tail_kernel, dims), out_shape=(jax.Shape...]
  transfers between devices with their start and end apart: 5 -> 3, of which waited for: 2 -> 1; matrix products, arithmetic and copies ran while one was open for 21% -> 35% of each run, Pallas kernels for 0% -> 0%
where the time goes in v1:
time: 196 us
  Pallas kernels  61.7 us (31%)
  other arithmetic  57 us (29%)
  matrix products  25.1 us (13%)
  local copies, waits for them, and re-layouts  15.7 us (8%)
  starting transfers between devices  13.5 us (7%)
  blocking collectives  11.1 us (6%)
  waiting for transfers between devices  11 us (6%)
    pallas_call x1, Pallas kernels, tail(): pl.pallas_call(functools.partial(tail_kernel, dims), out_shape=(jax.Shape...  61.7 us
    reduce_sum x1, other arithmetic, body(): hit_count = jnp.sum(matches, axis=1, dtype=jnp.float32)  47.8 us
    all_to_all x1, blocking collectives, body(): lax.all_to_all(request_ids, 'owner', split_axis=0, concat_axis=0, tiled=T...  11.1 us
    all_to_all x1, waiting for transfers between devices, body(): lax.all_to_all(slot_grads, 'owner', split_axis=0, concat_axis=0, tiled=True)  11 us
    dot_general x1, matrix products, body(): lax.dot_general(documents, inner_grad, (((0,), (0,)), ((), ())), preferre...  9.76 us
    scatter-add x1, other arithmetic, body(): owner_sum.at[flat_ids]  8.28 us
    dot_general x1, matrix products, body(): lax.dot_general(embedded, fetched, (((1,), (1,)), ((), ())), preferred_el...  7.53 us
    gather x1, local copies, waits for them, and re-layouts, body(): picked_scale = row_scale[flat_ids].reshape(owners, capacity)  6.25 us
  transfers between devices with their start and end apart: 3, of which 1 were waited for; matrix products, arithmetic and copies ran while one was open for 35% of the time, Pallas kernels for 0%

profile of v1, /device:TPU:1, one launch (start us, length us, event | category | flops | bytes accessed | tf_op | source)
XLA Modules:
  0.0 195.9 jit_solution(1890707567202880954)
XLA Ops:
  0.6 0.0 copy-start
  0.6 0.0 copy-start.3
  0.7 0.0 copy-start.1
  0.7 11.1 %all_to_all.28 = s32[8,1,128]{2,1,0:T(1,128)S(1)} all-to-all(s32[8,1,128]{2,1,0:T(1,128)} %bitcast.36), channel_id=1, replica_groups=mesh['owner'=8,'dp'=32] {'owner'}, dimensions={0} | all-to-all | bytes 8192 | tf_op jit(solution)/shard_map/all_to_all | solution.py:258
  11.8 6.2 %gather_fusion.1 = bf16[1024]{0:T(1024)(128)(2,1)S(1)} fusion(bf16[512]{0:T(512)(128)(2,1)} %param.11, s32[1024]{0:T(1024)S(1)} %broadcast_clamp_fusion), kind=kCustom, calls=%fused_computation.1 | custom fusion | bytes 8192 | tf_op jit(solution)/shard_map/gather | solution.py:261
  18.0 0.6 copy.18
  18.6 3.9 %all-to-all-start.2 = ((bf16[8,1,128]{2,1,0:T(2,128)(2,1)}), bf16[8,1,128]{2,1,0:T(2,128)(2,1)S(1)}, u32[]{:S(2)}, u32[]{:S(2)}) async-start(bf16[8,1,128]{2,1,0:T(2,128)(2,1)} %copy.18), calls=%async_computation.2 | async-start | bytes 8192 | tf_op jit(solution)/shard_map/all_to_all | solution.py:264
  22.5 0.9 convert_element_type.59
  23.4 0.2 copy.19
  23.6 0.0 copy-done.3
  23.7 0.2 copy.17
  23.9 0.0 copy-done.1
  23.9 5.2 %gather_fusion = bf16[1024,768]{1,0:T(8,128)(2,1)} fusion(bf16[512,768]{1,0:T(8,128)(2,1)S(1)} %copy-done.1, s32[1024]{0:T(1024)S(1)} %broadcast_clamp_fusion), kind=kCustom, calls=%fused_computation | custom fusion | bytes 3149824 | tf_op jit(solution)/shard_map/gather | solution.py:260
  29.1 0.0 all-to-all-done.2
  29.1 4.8 %all-to-all-start.1 = ((bf16[8,128,768]{2,1,0:T(8,128)(2,1)}), bf16[8,128,768]{2,1,0:T(8,128)(2,1)}, u32[]{:S(2)}, u32[]{:S(2)}) async-start(bf16[8,128,768]{2,1,0:T(8,128)(2,1)} %bitcast.5), calls=%async_computation.1 | async-start | bytes 3145728 | tf_op jit(solution)/shard_map/all_to_all | solution.py:263
  33.9 47.8 %convert_reduce_fusion = (f32[1024,1024]{1,0:T(8,128)}, f32[1024,1024]{1,0:T(8,128)}) fusion(s32[1024,32]{1,0:T(8,128)S(1)} %copy.17, f32[1024,32]{1,0:T(8,128)S(1)} %copy.19), kind=kLoop, calls=%fused_computation.4 | loop fusion | flops 199229440 | bytes 8650752 | tf_op jit(solution)/shard_map/reduce_sum | solution.py:280
  81.7 0.1 convert_bitcast_fusion
  81.7 0.0 copy-done
  81.7 4.7 %fusion.5 = f32[1024,768]{1,0:T(8,128)} fusion(bf16[1024,768]{1,0:T(8,128)(2,1)} %param.8, bf16[768,768]{1,0:T(8,128)(2,1)S(1)} %copy-done), kind=kOutput, calls=%fused_computation.20 | convolution fusion | flops 1207959552 | bytes 5898240 | tf_op jit(solution)/shard_map/dot_general | solution.py:255
  86.4 0.0 all-to-all-done.1
  86.4 7.5 %multiply_convert_fusion = bf16[1024,1024]{1,0:T(8,128)(2,1)S(1)} fusion(f32[1024,1024]{1,0:T(8,128)} %get-tuple-element.7, f32[1024,1024]{1,0:T(8,128)} %get-tuple-element.6, bf16[1024,768]{1,0:T(8,128)(2,1)} %bitcast.6, f32[1024]{0:T(1024)S(1)} %broadcast_multiply_fusion, f32[1024]{0:T(1024)S(1)} %bitcast.34, f32[1024]{0:T(1024)S(1)} %convert_bitcast_fusion, ...), kind=kOutput, calls=%fused_computation.6 | convolution fusion | flops 1622409216 | bytes 16789504 | tf_op jit(solution)/shard_map/dot_general | solution.py:268
  94.0 0.0 copy-done.6
  94.0 0.0 copy-start.7
  94.0 3.2 %convolution_convert_fusion = bf16[1024,768]{1,0:T(8,128)(2,1)} fusion(bf16[1024,1024]{1,0:T(8,128)(2,1)S(1)} %multiply_convert_fusion, bf16[1024,768]{1,0:T(8,128)(2,1)S(1)} %copy-done.5, f32[1024,768]{1,0:T(8,128)S(1)} %copy-done.6), kind=kOutput, calls=%fused_computation.11 | convolution fusion | flops 1613758464 | bytes 8388608 | tf_op jit(solution)/shard_map/dot_general | solution.py:284
  97.2 4.8 %all-to-all-start.3 = ((bf16[8,128,768]{2,1,0:T(8,128)(2,1)}), bf16[8,128,768]{2,1,0:T(8,128)(2,1)S(1)}, u32[]{:S(2)}, u32[]{:S(2)}) async-start(bf16[8,128,768]{2,1,0:T(8,128)(2,1)} %bitcast.30), calls=%async_computation.3 | async-start | bytes 3145728 | tf_op jit(solution)/shard_map/all_to_all | solution.py:288
  102.0 9.8 %fusion.3 = f32[768,768]{0,1:T(8,128)} fusion(bf16[1024,768]{1,0:T(8,128)(2,1)} %param.8, f32[1024,768]{1,0:T(8,128)} %fusion.5, bf16[1024,1024]{1,0:T(8,128)(2,1)} %copy-done.7, bf16[1024,768]{1,0:T(8,128)(2,1)} %bitcast.6), kind=kOutput, calls=%fused_computation.13 | convolution fusion | flops 2821718016 | bytes 10747904 | tf_op jit(solution)/shard_map/dot_general | solution.py:295
  111.7 11.0 %all-to-all-done.3 = bf16[8,128,768]{2,1,0:T(8,128)(2,1)S(1)} async-done(((bf16[8,128,768]{2,1,0:T(8,128)(2,1)}), bf16[8,128,768]{2,1,0:T(8,128)(2,1)S(1)}, u32[]{:S(2)}, u32[]{:S(2)}) %all-to-all-start.3) | async-done | bytes 1572896 | tf_op jit(solution)/shard_map/all_to_all | solution.py:288
  122.7 1.1 copy-done.2
  123.8 8.3 %scatter_custom_fusion = f32[512,768]{1,0:T(8,128)S(1)} fusion(s32[1024]{0:T(1024)S(1)} %bitcast.32, bf16[1024,768]{1,0:T(8,128)(2,1)} %bitcast.28, f32[]{:T(128)} %constant.5.clone.1), kind=kCustom, calls=%fused_computation.7 | custom fusion | flops 1572864 | bytes 3145732 | tf_op jit(solution)/shard_map/scatter-add | solution.py:290
  132.1 61.7 %reduce_gradients.1 = (f32[16,768]{1,0:T(8,128)S(1)}, f32[2,384,768]{2,1,0:T(8,128)S(1)}) custom-call(f32[8,4,16,768]{3,2,1,0:T(8,128)S(1)} %bitcast.26, f32[2,384,768]{2,1,0:T(8,128)} %bitcast.29), custom_call_target="tpu_custom_call" | custom-call | flops 100000000 | bytes 10000000 | tf_op jit(solution)/shard_map/reduce_gradients/pallas_call | solution.py:213
  193.9 0.6 copy.22
  194.5 1.4 copy.23
  (11 shorter events, 0.0 us)
Async XLA Ops:
  0.6 81.1 %copy-start = (bf16[768,768]{1,0:T(8,128)(2,1)S(1)}, bf16[768,768]{1,0:T(8,128)(2,1)}, u32[]{:S(2)}) copy-start(bf16[768,768]{1,0:T(8,128)(2,1)} %param.9) | copy-start | bytes 3538948
  0.6 23.0 %copy-start.3 = (s32[1024,32]{0,1:T(8,128)S(1)}, s32[1024,32]{0,1:T(8,128)}, u32[]{:S(2)}) copy-start(s32[1024,32]{0,1:T(8,128)} %param.12) | copy-start | bytes 393220
  0.7 23.2 %copy-start.1 = (bf16[512,768]{1,0:T(8,128)(2,1)S(1)}, bf16[512,768]{1,0:T(8,128)(2,1)}, u32[]{:S(2)}) copy-start(bf16[512,768]{1,0:T(8,128)(2,1)} %param.10) | copy-start | bytes 2359300
  18.6 10.5 %all-to-all-start.2 = ((bf16[8,1,128]{2,1,0:T(2,128)(2,1)}), bf16[8,1,128]{2,1,0:T(2,128)(2,1)S(1)}, u32[]{:S(2)}, u32[]{:S(2)}) async-start(bf16[8,1,128]{2,1,0:T(2,128)(2,1)} %copy.18), calls=%async_computation.2 | async-start | bytes 8192 | tf_op jit(solution)/shard_map/all_to_all | solution.py:264
  29.1 57.3 %all-to-all-start.1 = ((bf16[8,128,768]{2,1,0:T(8,128)(2,1)}), bf16[8,128,768]{2,1,0:T(8,128)(2,1)}, u32[]{:S(2)}, u32[]{:S(2)}) async-start(bf16[8,128,768]{2,1,0:T(8,128)(2,1)} %bitcast.5), calls=%async_computation.1 | async-start | bytes 3145728 | tf_op jit(solution)/shard_map/all_to_all | solution.py:263
  33.9 47.8 %copy-start.4 = (s32[1,8]{1,0:T(1,128)S(1)}, s32[1,8]{1,0:T(1,128)}, u32[]{:S(2)}) copy-start(s32[1,8]{1,0:T(1,128)} %param.15) | copy-start | bytes 100
  81.7 4.7 %copy-start.5 = (bf16[1024,768]{1,0:T(8,128)(2,1)S(1)}, bf16[1024,768]{1,0:T(8,128)(2,1)}, u32[]{:S(2)}) copy-start(bf16[1024,768]{1,0:T(8,128)(2,1)} %param.8) | copy-start | bytes 4718596
  86.4 7.6 %copy-start.6 = (f32[1024,768]{1,0:T(8,128)S(1)}, f32[1024,768]{1,0:T(8,128)}, u32[]{:S(2)}) copy-start(f32[1024,768]{1,0:T(8,128)} %fusion.5) | copy-start | bytes 9437188
  94.0 3.2 %copy-start.7 = (bf16[1024,1024]{1,0:T(8,128)(2,1)}, bf16[1024,1024]{1,0:T(8,128)(2,1)S(1)}, u32[]{:S(2)}) copy-start(bf16[1024,1024]{1,0:T(8,128)(2,1)S(1)} %multiply_convert_fusion) | copy-start | bytes 6291460
  97.2 25.5 %all-to-all-start.3 = ((bf16[8,128,768]{2,1,0:T(8,128)(2,1)}), bf16[8,128,768]{2,1,0:T(8,128)(2,1)S(1)}, u32[]{:S(2)}, u32[]{:S(2)}) async-start(bf16[8,128,768]{2,1,0:T(8,128)(2,1)} %bitcast.30), calls=%async_computation.3 | async-start | bytes 3145728 | tf_op jit(solution)/shard_map/all_to_all | solution.py:288
  122.7 1.1 copy-start.2

commit v2 on v0

v2 whole, which is shorter than its diff:
```python
import functools

import jax
import jax.numpy as jnp
from jax import lax
from jax.experimental import pallas as pl
from jax.experimental.pallas import tpu as pltpu
from jax.sharding import PartitionSpec as P

MESH = pl.DeviceIdType.MESH
F32 = jnp.float32
BF16 = jnp.bfloat16
I32 = jnp.int32


def torus(mesh):
    owners, groups = mesh.shape["owner"], mesh.shape["dp"]
    ny = 4 if groups >= 16 else 2
    return owners // 2, ny, groups // ny


def remote(src, dst, send, recv, target):
    return pltpu.make_async_remote_copy(
        src_ref=src, dst_ref=dst, send_sem=send, recv_sem=recv, device_id=target, device_id_type=MESH
    )


def step_kernel(
    dims, docs, weight, slab, scale, ids, slots, marks, counts, slab_out, enc_out,
    emb, slope, onehot, srows, frows, sscale, fscale, gids, tally, dscore, grads, back,
    own, ownb, gota, gotb, acca, accb, gota2, gotb2,
    inner, enc, sib, accp, accq, gotp, gotq, allp, allq,
    s_id, r_id, s_f, r_f, s_c, r_c, s_g, r_g,
    s_a, r_a, s_b, r_b, s_a2, r_a2, s_b2, r_b2,
    s_sib, r_sib, s_p, r_p, s_q, r_q, s_p2, r_p2, s_q2, r_q2, s_p3, r_p3, s_q3, r_q3, s_e, r_e,
):
    nx, ny, nz = dims
    owner, group = lax.axis_index("owner"), lax.axis_index("dp")
    x, c = owner // 2, owner % 2
    y, z = group % ny, group // ny
    here = x * ny + y
    owners = 2 * nx
    cap = srows.shape[1]
    pair = 2 * cap
    documents, width = docs.shape
    rows_held = slab.shape[0]
    wide = gota.shape[-1]
    depth = gota.shape[-2]
    piece = accp.shape[1]
    half = enc.shape[1]
    cut = nx * ny * piece
    tile = min(256, documents)

    plane = [(i, j) for i in range(nx) for j in range(ny) if (i, j) != (0, 0)]
    rings = list(range(1, nz))
    cols = list(range(1, ny))

    def chip(i, j, k, core):
        return {"owner": lax.rem(x + i, nx) * 2 + core, "dp": lax.rem(z + k, nz) * ny + lax.rem(y + j, ny)}

    def spread(r):
        return r + (r // 2) * (5 - 2 * r) if nx == 4 else r

    bar = pltpu.get_barrier_semaphore()
    greeted = 0
    for i, j in plane:
        pl.semaphore_signal(bar, inc=1, device_id=chip(i, j, 0, c), device_id_type=MESH)
        greeted += 1
    for i in range(nx):
        pl.semaphore_signal(bar, inc=1, device_id=chip(i, 0, 0, 1 - c), device_id_type=MESH)
        greeted += 1
    for k in rings:
        pl.semaphore_signal(bar, inc=1, device_id=chip(0, 0, k, c), device_id_type=MESH)
        greeted += 1
    pl.semaphore_wait(bar, greeted)

    def peer(n):
        r, flip = n // 2, n % 2
        core = lax.rem(c + flip, 2)
        to = lax.rem(x + spread(r), nx) * 2 + core
        source = lax.rem(x + nx - spread(r), nx) * 2 + core
        return to, source

    def id_copy(n):
        to, _ = peer(n)
        return remote(ids.at[to], gids.at[owner], s_id.at[n], r_id.at[n], {"owner": to, "dp": group})

    for n in range(1, owners):
        id_copy(n).start()
    gids[owner] = ids[owner]

    def encode(t, _):
        rows = pl.ds(pl.multiple_of(t * tile, tile), tile)
        block = docs[rows, :]
        squashed = jnp.tanh(jnp.dot(block, weight[...], preferred_element_type=F32))
        emb[rows, :] = (block.astype(F32) + squashed).astype(BF16)
        slope[rows, :] = 1.0 - squashed * squashed
        return 0

    lax.fori_loop(0, documents // tile, encode, 0)

    def row_copy(n):
        to, _ = peer(n)
        return remote(srows.at[to], frows.at[owner], s_f.at[n], r_f.at[n], {"owner": to, "dp": group})

    def scale_copy(n):
        to, _ = peer(n)
        return remote(sscale.at[to], fscale.at[owner], s_c.at[n], r_c.at[n], {"owner": to, "dp": group})

    scale_rows = jnp.broadcast_to(scale[...].astype(BF16), (16, rows_held))

    def serve(n, _):
        to, _source = peer(n)

        @pl.when(n > 0)
        def _():
            id_copy(n).wait_send()

        hot = jnp.where(
            lax.broadcasted_iota(I32, (rows_held, cap), 0) == gids[to], 1.0, 0.0
        ).astype(BF16)
        onehot[:, pl.ds(pl.multiple_of(to * cap, cap), cap)] = hot
        rows = lax.dot_general(hot, slab[...], (((0,), (0,)), ((), ())), preferred_element_type=F32).astype(BF16)
        sc = jnp.dot(scale_rows, hot, preferred_element_type=F32).astype(BF16)
        srows[to] = rows
        sscale[to] = sc

        @pl.when(n == 0)
        def _():
            frows[owner] = rows
            fscale[owner] = sc

        @pl.when(n > 0)
        def _():
            row_copy(n).start()
            scale_copy(n).start()

        return 0

    for n in range(1, owners):
        id_copy(n).wait_recv()
    lax.fori_loop(0, owners, serve, 0)

    def grad_copy(n):
        _, source = peer(n)
        return remote(grads.at[source], back.at[owner], s_g.at[n], r_g.at[n], {"owner": source, "dp": group})

    bits = 64
    strip = 64

    def score(r, _):
        first = lax.rem(x + nx - spread(r), nx) * 2
        base = first * cap

        def count(m, _):
            low = pl.multiple_of((m // (documents // tile)) * strip, strip)
            lanes = pl.ds(pl.multiple_of((m % (documents // tile)) * tile, tile), tile)
            index = lax.broadcasted_iota(I32, (strip, tile), 0) + (base + low)
            total = jnp.zeros((strip, tile), I32)
            for k in range(slots.shape[0]):
                total += jnp.where(slots[k : k + 1, lanes] == index, marks[k : k + 1, lanes], 0)
            tally[pl.ds(low, strip), lanes] = total
            return 0

        lax.fori_loop(0, (pair // strip) * (documents // tile), count, 0)

        @pl.when(r > 0)
        def _():
            row_copy(2 * r).wait()
            scale_copy(2 * r).wait()

        row_copy(2 * r + 1).wait()
        scale_copy(2 * r + 1).wait()

        rows = frows[pl.ds(first, 2)].reshape(pair, width)
        factor, live = [], []
        for q in range(2):
            line = fscale[first + q].astype(F32)[0:1]
            factor.append(jnp.broadcast_to(line, (cap, cap)).T[:, 0:1])
            live.append(jnp.where(lax.broadcasted_iota(I32, (cap, 1), 0) < counts[0, first + q], 1.0, 0.0))
        factor = jnp.concatenate(factor, axis=0)
        live = jnp.concatenate(live, axis=0)

        def slice_of(t, _):
            lanes = pl.ds(pl.multiple_of(t * tile, tile), tile)
            logits = lax.dot_general(
                rows, emb[lanes, :], (((1,), (1,)), ((), ())), preferred_element_type=F32
            ) * factor
            chance = 0.5 * jnp.tanh(0.5 * logits) + 0.5
            mark = tally[:, lanes]
            hits = (mark & (bits - 1)).astype(F32)
            on = (mark >> 6).astype(F32)
            dlogit = ((hits + live) * chance - on) * (1.0 / slots.shape[0])
            dscore[pl.ds(pl.multiple_of(base, cap), pair), lanes] = (dlogit * factor).astype(BF16)
            return 0

        lax.fori_loop(0, documents // tile, slice_of, 0)
        mine = dscore[pl.ds(pl.multiple_of(base, cap), pair), :]
        grads[pl.ds(first, 2)] = jnp.dot(mine, emb[...], preferred_element_type=F32).astype(BF16).reshape(2, cap, width)

        @pl.when(r > 0)
        def _():
            grad_copy(2 * r).start()

        grad_copy(2 * r + 1).start()
        return 0

    lax.fori_loop(0, nx, score, 0)
    back[owner] = grads[owner]

    table = frows[...].reshape(owners * cap, width)

    def pull(t, _):
        rows = pl.ds(pl.multiple_of(t * tile, tile), tile)
        emb_grad = lax.dot_general(
            dscore[:, rows], table, (((0,), (0,)), ((), ())), preferred_element_type=F32
        )
        inner[rows, :] = (emb_grad * slope[rows, :]).astype(BF16)
        return 0

    lax.fori_loop(0, documents // tile, pull, 0)

    def outer(which):
        side = docs[:, pl.ds(pl.multiple_of(which * half, half), half)]
        enc[which] = lax.dot_general(side, inner[...], (((0,), (0,)), ((), ())), preferred_element_type=F32)

    outer(1 - c)
    swap = remote(enc.at[1 - c], sib, s_sib, r_sib, chip(0, 0, 0, 1 - c))
    swap.start()
    outer(c)
    swap.wait()

    def join_p(q, _):
        rows = pl.ds(pl.multiple_of(q * piece, piece), piece)
        accp[q] = (enc[c, rows, :] + sib[rows, :]).astype(BF16)
        return 0

    def join_q(q, _):
        rows = pl.ds(pl.multiple_of(cut + q * piece, piece), piece)
        accq[q] = (enc[c, rows, :] + sib[rows, :]).astype(BF16)
        return 0

    lax.fori_loop(0, nx * ny, join_p, 0)
    lax.fori_loop(0, nz, join_q, 0)
    p1, q1 = [], []
    for n, (i, j) in enumerate(plane):
        to = lax.rem(x + i, nx) * ny + lax.rem(y + j, ny)
        p1.append(remote(accp.at[to], gotp.at[n], s_p.at[n], r_p.at[n], chip(i, j, 0, c)))
    for k in rings:
        to = lax.rem(z + k, nz)
        q1.append(remote(accq.at[to], gotq.at[k - 1], s_q.at[k - 1], r_q.at[k - 1], chip(0, 0, k, c)))
    for copy in p1 + q1:
        copy.start()

    for copy in p1:
        copy.wait()
    rows = pl.ds(pl.multiple_of(here * piece, piece), piece)
    total = enc[c, rows, :] + sib[rows, :]
    for n in range(len(plane)):
        total += gotp[n].astype(F32)
    allp[z] = total
    p2, q2 = [], []
    for k in rings:
        p2.append(remote(allp.at[z], allp.at[z], s_p2.at[k - 1], r_p2.at[k - 1], chip(0, 0, k, c)))
    for copy in p2:
        copy.start()
    for copy in q1:
        copy.wait()
    rows = pl.ds(pl.multiple_of(cut + z * piece, piece), piece)
    total = enc[c, rows, :] + sib[rows, :]
    for k in rings:
        total += gotq[k - 1].astype(F32)
    allq[here] = total
    for n, (i, j) in enumerate(plane):
        q2.append(remote(allq.at[here], allq.at[here], s_q2.at[n], r_q2.at[n], chip(i, j, 0, c)))
    for copy in q2:
        copy.start()

    for n in range(1, owners):
        grad_copy(n).wait()
    returned = back[...].reshape(owners * cap, width)
    span = ny * depth

    def gather_rows(k, _):
        rows = pl.ds(pl.multiple_of(k * span, span), span)
        total = jnp.dot(onehot[rows, :], returned, preferred_element_type=F32).reshape(ny, depth, width)
        own[k] = total
        ownb[k] = total.astype(BF16)
        return 0

    lax.fori_loop(0, nz, gather_rows, 0)
    first_a, first_b, second_a, second_b = [], [], [], []
    for j in cols:
        py = lax.rem(y + j, ny)
        first_a.append(remote(ownb.at[:, py, :, 0:wide], gota.at[j - 1], s_a.at[j - 1], r_a.at[j - 1],
                              chip(0, j, 0, c)))
    for k in rings:
        pz = lax.rem(z + k, nz)
        first_b.append(remote(ownb.at[pz, :, :, wide:], gotb.at[k - 1], s_b.at[k - 1], r_b.at[k - 1],
                              chip(0, 0, k, c)))
    for copy in first_a + first_b:
        copy.start()

    p3, q3 = [], []
    for copy in p2:
        copy.wait()
    total = allp[0]
    for k in range(1, nz):
        total += allp[k]
    rows_p = pl.ds(pl.multiple_of(here * piece, piece), piece)
    enc_out[c, rows_p, :] = total
    for n, (i, j) in enumerate(plane):
        part = enc_out.at[c, rows_p, :]
        p3.append(remote(part, part, s_p3.at[n], r_p3.at[n], chip(i, j, 0, c)))
    for copy in p3:
        copy.start()
    for copy in q2:
        copy.wait()
    total = allq[0]
    for k in range(1, nx * ny):
        total += allq[k]
    rows_q = pl.ds(pl.multiple_of(cut + z * piece, piece), piece)
    enc_out[c, rows_q, :] = total
    for k in rings:
        part = enc_out.at[c, rows_q, :]
        q3.append(remote(part, part, s_q3.at[k - 1], r_q3.at[k - 1], chip(0, 0, k, c)))
    for copy in q3:
        copy.start()

    for copy in first_a:
        copy.wait()

    def join_a(q, _):
        total = own[q, y, :, 0:wide]
        for j in cols:
            total += gota[j - 1, q].astype(F32)
        acca[q] = total
        return 0

    lax.fori_loop(0, nz, join_a, 0)
    for k in rings:
        pz = lax.rem(z + k, nz)
        second_a.append(remote(acca.at[pz], gota2.at[k - 1], s_a2.at[k - 1], r_a2.at[k - 1], chip(0, 0, k, c)))
    for copy in second_a:
        copy.start()
    for copy in first_b:
        copy.wait()

    def join_b(q, _):
        total = own[z, q, :, wide:]
        for k in rings:
            total += gotb[k - 1, q].astype(F32)
        accb[q] = total
        return 0

    lax.fori_loop(0, ny, join_b, 0)
    for j in cols:
        py = lax.rem(y + j, ny)
        second_b.append(remote(accb.at[py], gotb2.at[j - 1], s_b2.at[j - 1], r_b2.at[j - 1], chip(0, j, 0, c)))
    for copy in second_b:
        copy.start()

    for copy in p3:
        copy.wait()
    upper = enc_out.at[c, 0:cut, :]
    lower = enc_out.at[c, cut:half, :]
    last_p = remote(upper, upper, s_e.at[0], r_e.at[0], chip(0, 0, 0, 1 - c))
    last_p.start()
    for copy in q3:
        copy.wait()
    last_q = remote(lower, lower, s_e.at[1], r_e.at[1], chip(0, 0, 0, 1 - c))
    last_q.start()

    for copy in second_a:
        copy.wait()
    total = acca[z]
    for k in rings:
        total += gota2[k - 1]
    slab_out[:, 0:wide] = total
    for copy in second_b:
        copy.wait()
    total = accb[y]
    for j in cols:
        total += gotb2[j - 1]
    slab_out[:, wide:] = total
    last_p.wait()
    last_q.wait()


def body(dims, documents, enc_weight, label_slab, row_scale, shortlist, positive, request_ids, counts):
    nx, ny, nz = dims
    docs, width = documents.shape
    held = label_slab.shape[0]
    owners, cap = request_ids.shape
    plane = nx * ny
    depth = held // (ny * nz)
    wide = 2 * width // 3
    slim = width - wide
    half = width // 2
    piece = half // (plane + nz)
    slot_count = owners * cap
    f32 = lambda *shape: pltpu.VMEM(shape, F32)
    b16 = lambda *shape: pltpu.VMEM(shape, BF16)
    i32 = lambda *shape: pltpu.VMEM(shape, I32)
    dma = lambda n: [pltpu.SemaphoreType.DMA((n,))] * 2
    vmem = pl.BlockSpec(memory_space=pltpu.VMEM)
    slab_grad, enc_grad = pl.pallas_call(
        functools.partial(step_kernel, dims),
        out_shape=(jax.ShapeDtypeStruct((depth, width), F32), jax.ShapeDtypeStruct((2, half, width), F32)),
        in_specs=[vmem] * 7 + [pl.BlockSpec(memory_space=pltpu.SMEM)],
        out_specs=[vmem] * 2,
        scratch_shapes=[
            b16(docs, width), f32(docs, width), b16(held, slot_count),
            b16(owners, cap, width), b16(owners, cap, width),
            b16(owners, 16, cap), b16(owners, 16, cap), i32(owners, 1, cap),
            i32(2 * cap, docs), b16(slot_count, docs),
            b16(owners, cap, width), b16(owners, cap, width),
            f32(nz, ny, depth, width), b16(nz, ny, depth, width),
            b16(ny - 1, nz, depth, wide), b16(nz - 1, ny, depth, slim),
            f32(nz, depth, wide), f32(ny, depth, slim),
            f32(nz - 1, depth, wide), f32(ny - 1, depth, slim),
            b16(docs, width), f32(2, half, width), f32(half, width),
            b16(plane, piece, width), b16(nz, piece, width),
            b16(plane - 1, piece, width), b16(nz - 1, piece, width),
            f32(nz, piece, width), f32(plane, piece, width),
            *dma(owners), *dma(owners), *dma(owners), *dma(owners),
            *dma(ny - 1), *dma(nz - 1), *dma(nz - 1), *dma(ny - 1),
            pltpu.SemaphoreType.DMA, pltpu.SemaphoreType.DMA,
            *dma(plane - 1), *dma(nz - 1), *dma(nz - 1), *dma(plane - 1), *dma(plane - 1), *dma(nz - 1),
            *dma(2),
        ],
        compiler_params=pltpu.CompilerParams(
            collective_id=1, has_side_effects=True, vmem_limit_bytes=56 * 2**20
        ),
        cost_estimate=pl.CostEstimate(flops=10**10, bytes_accessed=10**7, transcendentals=2 * 10**6),
        name="classifier_step",
    )(
        documents,
        enc_weight,
        label_slab,
        row_scale.reshape(1, held),
        request_ids.reshape(owners, 1, cap),
        shortlist.T,
        (1 + 64 * positive).T,
        counts,
    )
    return slab_grad, enc_grad.reshape(width, width)


def solution(mesh):
    return jax.shard_map(
        functools.partial(body, torus(mesh)),
        mesh=mesh,
        in_specs=(
            P(("owner", "dp"), None),
            P(),
            P("owner", None),
            P("owner"),
            P(("owner", "dp"), None),
            P(("owner", "dp"), None),
            P(("owner", "dp"), None),
            P(("owner", "dp"), None),
        ),
        out_specs=(P(("owner", "dp"), None), P()),
        check_vma=False,
    )
```

time: 394 us -> 103 us (0.26)
  waiting for transfers between devices: 254 us -> 0 us
  Pallas kernels: 0 us -> 93.5 us
  other arithmetic: 57.3 us -> 1.57 us
  matrix products: 25.4 us -> 0 us
  between operations: 15.6 us -> 0.64 us
  starting transfers between devices: 13.6 us -> 0 us
  blocking collectives: 11.1 us -> 0 us
  local copies, waits for them, and re-layouts: 15.5 us -> 5.9 us
    psum x1 -> x0, waiting for transfers between devices: 244 us -> none  [body(): enc_grad = lax.psum(enc_local, ('owner', 'dp'))]
    pallas_call x0 -> x1, Pallas kernels: none -> 93.5 us  [body(): pl.pallas_call(functools.partial(step_kernel, dims), out_shape=(jax.Shape...]
    reduce_sum x1 -> x0, other arithmetic: 47.7 us -> none  [body(): hit_count = jnp.sum(matches, axis=1, dtype=jnp.float32)]
    dot_general x4 -> x0, matrix products: 25.4 us -> none  [the longest x1 10.1 us: body(): lax.dot_general(documents, inner_grad, (((0,), (0,)), ((), ())), preferre...]
    all_to_all x3 -> x0, starting transfers between devices: 13.5 us -> none  [the longest x1 4.82 us: body(): lax.all_to_all(picked, 'owner', split_axis=0, concat_axis=0, tiled=True)]
    gather x2 -> x0, local copies, waits for them, and re-layouts: 11.5 us -> none  [the longest x1 6.25 us: body(): picked_scale = row_scale[flat_ids].reshape(owners, capacity)]
    all_to_all x1 -> x0, blocking collectives: 11.1 us -> none  [body(): lax.all_to_all(request_ids, 'owner', split_axis=0, concat_axis=0, tiled=T...]
    all_to_all x3 -> x0, waiting for transfers between devices: 10.6 us -> none  [the longest x1 10.6 us: body(): lax.all_to_all(slot_grads, 'owner', split_axis=0, concat_axis=0, tiled=True)]
  transfers between devices with their start and end apart: 5 -> 0, of which waited for: 2 -> 0; matrix products, arithmetic and copies ran while one was open for 21% -> 0% of each run, Pallas kernels for 0% -> 0%
where the time goes in v2:
time: 103 us; the launch traced here: 102 us
  Pallas kernels  93.5 us (91%)
  local copies, waits for them, and re-layouts  5.9 us (6%)
  other arithmetic  1.57 us (2%)
    pallas_call x1, Pallas kernels, body(): pl.pallas_call(functools.partial(step_kernel, dims), out_shape=(jax.Shape...  93.5 us
    unnamed x2, local copies, waits for them, and re-layouts  4.64 us

profile of v2, /device:TPU:1, one launch (start us, length us, event | category | flops | bytes accessed | tf_op | source)
XLA Modules:
  0.0 101.6 jit_solution(9798396860531138994)
XLA Ops:
  0.6 1.3 %reshape.13.scale = bf16[1,512]{1,0:T(2,128)(2,1)} reshape(bf16[512]{0:T(512)(128)(2,1)} %param.11) | data formatting | bytes 2048 | tf_op jit(solution)/shard_map/reshape | solution.py:441
  1.9 1.6 %add_bitcast_fusion.marks = s32[32,1024]{1,0:T(8,128)} fusion(s32[1024,32]{0,1:T(8,128)} %param.13), kind=kLoop, calls=%fused_computation | loop fusion | flops 65536 | bytes 262144 | tf_op jit(solution)/shard_map/transpose | solution.py:444
  3.5 93.5 %classifier_step.1 = (f32[16,768]{1,0:T(8,128)}, f32[2,384,768]{2,1,0:T(8,128)}) custom-call(bf16[1024,768]{1,0:T(8,128)(2,1)} %docs.1, bf16[768,768]{1,0:T(8,128)(2,1)} %weight.1, bf16[512,768]{1,0:T(8,128)(2,1)} %slab.1, bf16[1,512]{1,0:T(2,128)(2,1)} %reshape.13.scale, s32[8,1,128]{2,1,0:T(1,128)} %bitcast.7, s32[32,1024]{1,0:T(8,128)} %bitcast.6, ...), custom_call_target="tpu_custom_call" | custom-call | flops 10000000000 | bytes 10000000 | tf_op jit(solution)/shard_map/classifier_step/pallas_call | solution.py:407
  97.0 1.4 %copy.12 = f32[16,768]{1,0:T(8,128)} copy(f32[16,768]{1,0:T(8,128)} %get-tuple-element.8) | data formatting | bytes 98304
  98.4 3.2 %copy.13 = f32[768,768]{1,0:T(8,128)} copy(f32[768,768]{1,0:T(8,128)} %bitcast.5) | data formatting | bytes 4718592

commit v3 on v2

--- a/solution.py
+++ b/solution.py
@@ -11,6 +11,7 @@
 F32 = jnp.float32
 BF16 = jnp.bfloat16
 I32 = jnp.int32
+I16 = jnp.int16
 
 
 def torus(mesh):
@@ -26,11 +27,11 @@
 
 
 def step_kernel(
-    dims, docs, weight, slab, scale, ids, slots, marks, counts, slab_out, enc_out,
-    emb, slope, onehot, srows, frows, sscale, fscale, gids, tally, dscore, grads, back,
+    dims, docs_in, weight_in, slab_in, scale, ids, slots_in, on_in, counts, slab_out, enc_out,
+    docs, weight, slab, slots32, on32, slots, marks, emb, slope, push, onehot, srows, frows, sscale, fscale, gids, tally, dscore, grads, back,
     own, ownb, gota, gotb, acca, accb, gota2, gotb2,
     inner, enc, sib, accp, accq, gotp, gotq, allp, allq,
-    s_id, r_id, s_f, r_f, s_c, r_c, s_g, r_g,
+    s_in, s_id, r_id, s_f, r_f, s_c, r_c, s_g, r_g,
     s_a, r_a, s_b, r_b, s_a2, r_a2, s_b2, r_b2,
     s_sib, r_sib, s_p, r_p, s_q, r_q, s_p2, r_p2, s_q2, r_q2, s_p3, r_p3, s_q3, r_q3, s_e, r_e,
 ):
@@ -49,7 +50,7 @@
     piece = accp.shape[1]
     half = enc.shape[1]
     cut = nx * ny * piece
-    tile = min(256, documents)
+    strip = min(128, documents)
 
     plane = [(i, j) for i in range(nx) for j in range(ny) if (i, j) != (0, 0)]
     rings = list(range(1, nz))
@@ -60,6 +61,15 @@
 
     def spread(r):
         return r + (r // 2) * (5 - 2 * r) if nx == 4 else r
+
+    loads = [
+        pltpu.make_async_copy(src, dst, s_in.at[n])
+        for n, (src, dst) in enumerate(
+            ((docs_in, docs), (weight_in, weight), (slab_in, slab), (slots_in, slots32), (on_in, on32))
+        )
+    ]
+    for load in loads:
+        load.start()
 
     bar = pltpu.get_barrier_semaphore()
     greeted = 0
@@ -89,15 +99,12 @@
         id_copy(n).start()
     gids[owner] = ids[owner]
 
-    def encode(t, _):
-        rows = pl.ds(pl.multiple_of(t * tile, tile), tile)
-        block = docs[rows, :]
-        squashed = jnp.tanh(jnp.dot(block, weight[...], preferred_element_type=F32))
-        emb[rows, :] = (block.astype(F32) + squashed).astype(BF16)
-        slope[rows, :] = 1.0 - squashed * squashed
-        return 0
-
-    lax.fori_loop(0, documents // tile, encode, 0)
+    loads[0].wait()
+    loads[1].wait()
+    squashed = jnp.tanh(jnp.dot(docs[...], weight[...], preferred_element_type=F32))
+    emb[...] = (docs[...].astype(F32) + squashed).astype(BF16)
+    slope[...] = 1.0 - squashed * squashed
+    loads[2].wait()
 
     def row_copy(n):
         to, _ = peer(n)
@@ -107,9 +114,10 @@
         to, _ = peer(n)
         return remote(sscale.at[to], fscale.at[owner], s_c.at[n], r_c.at[n], {"owner": to, "dp": group})
 
-    scale_rows = jnp.broadcast_to(scale[...].astype(BF16), (16, rows_held))
-
-    def serve(n, _):
+    scale_rows = jnp.broadcast_to(scale[...].reshape(1, rows_held), (16, rows_held))
+
+    def serve(m, _):
+        n = lax.rem(m + 2, owners)
         to, _source = peer(n)
 
         @pl.when(n > 0)
@@ -145,33 +153,30 @@
         _, source = peer(n)
         return remote(grads.at[source], back.at[owner], s_g.at[n], r_g.at[n], {"owner": source, "dp": group})
 
-    bits = 64
-    strip = 64
-
-    def score(r, _):
+    loads[3].wait()
+    loads[4].wait()
+    slots[...] = slots32[...].astype(I16)
+    marks[...] = (1 + 64 * on32[...]).astype(I16)
+    strips = documents // strip
+
+    def count(m, _):
+        base = pl.multiple_of((m // strips) * pair, pair)
+        lanes = pl.ds(pl.multiple_of((m % strips) * strip, strip), strip)
+        index = (lax.broadcasted_iota(I32, (pair, strip), 0) + base).astype(I16)
+        total = jnp.zeros((pair, strip), I16)
+        for k in range(slots.shape[0]):
+            total += jnp.where(slots[k : k + 1, lanes] == index, marks[k : k + 1, lanes], jnp.int16(0))
+        tally[pl.ds(base, pair), lanes] = total
+        return 0
+
+    lax.fori_loop(0, nx * strips, count, 0)
+
+    def group_of(r):
         first = lax.rem(x + nx - spread(r), nx) * 2
-        base = first * cap
-
-        def count(m, _):
-            low = pl.multiple_of((m // (documents // tile)) * strip, strip)
-            lanes = pl.ds(pl.multiple_of((m % (documents // tile)) * tile, tile), tile)
-            index = lax.broadcasted_iota(I32, (strip, tile), 0) + (base + low)
-            total = jnp.zeros((strip, tile), I32)
-            for k in range(slots.shape[0]):
-                total += jnp.where(slots[k : k + 1, lanes] == index, marks[k : k + 1, lanes], 0)
-            tally[pl.ds(low, strip), lanes] = total
-            return 0
-
-        lax.fori_loop(0, (pair // strip) * (documents // tile), count, 0)
-
-        @pl.when(r > 0)
-        def _():
-            row_copy(2 * r).wait()
-            scale_copy(2 * r).wait()
-
-        row_copy(2 * r + 1).wait()
-        scale_copy(2 * r + 1).wait()
-
+        return first, pl.ds(pl.multiple_of(first * cap, pair), pair)
+
+    def score(r):
+        first, span = group_of(r)
         rows = frows[pl.ds(first, 2)].reshape(pair, width)
         factor, live = [], []
         for q in range(2):
@@ -180,45 +185,56 @@
             live.append(jnp.where(lax.broadcasted_iota(I32, (cap, 1), 0) < counts[0, first + q], 1.0, 0.0))
         factor = jnp.concatenate(factor, axis=0)
         live = jnp.concatenate(live, axis=0)
-
-        def slice_of(t, _):
-            lanes = pl.ds(pl.multiple_of(t * tile, tile), tile)
-            logits = lax.dot_general(
-                rows, emb[lanes, :], (((1,), (1,)), ((), ())), preferred_element_type=F32
-            ) * factor
-            chance = 0.5 * jnp.tanh(0.5 * logits) + 0.5
-            mark = tally[:, lanes]
-            hits = (mark & (bits - 1)).astype(F32)
-            on = (mark >> 6).astype(F32)
-            dlogit = ((hits + live) * chance - on) * (1.0 / slots.shape[0])
-            dscore[pl.ds(pl.multiple_of(base, cap), pair), lanes] = (dlogit * factor).astype(BF16)
-            return 0
-
-        lax.fori_loop(0, documents // tile, slice_of, 0)
-        mine = dscore[pl.ds(pl.multiple_of(base, cap), pair), :]
-        grads[pl.ds(first, 2)] = jnp.dot(mine, emb[...], preferred_element_type=F32).astype(BF16).reshape(2, cap, width)
+        logits = lax.dot_general(rows, emb[...], (((1,), (1,)), ((), ())), preferred_element_type=F32) * factor
+        chance = 0.5 * jnp.tanh(0.5 * logits) + 0.5
+        mark = tally[span, :].astype(I32)
+        hits = (mark & 63).astype(F32)
+        on = (mark >> 6).astype(F32)
+        dlogit = ((hits + live) * chance - on) * (1.0 / slots.shape[0])
+        dscore[span, :] = (dlogit * factor).astype(BF16)
+
+    def row_grads(r):
+        first, span = group_of(r)
+        grads[pl.ds(first, 2)] = (
+            jnp.dot(dscore[span, :], emb[...], preferred_element_type=F32).astype(BF16).reshape(2, cap, width)
+        )
+
+    def pulled(r):
+        first, span = group_of(r)
+        rows = frows[pl.ds(first, 2)].reshape(pair, width)
+        return lax.dot_general(dscore[span, :], rows, (((0,), (0,)), ((), ())), preferred_element_type=F32)
+
+    def arrived(n):
+        row_copy(n).wait()
+        scale_copy(n).wait()
+
+    push[...] = jnp.zeros_like(push)
+
+    def work(r, _):
+        @pl.when(r > 0)
+        def _():
+            arrived(2 * r)
+
+        arrived(2 * r + 1)
+        score(r)
+        row_grads(r)
 
         @pl.when(r > 0)
         def _():
             grad_copy(2 * r).start()
 
         grad_copy(2 * r + 1).start()
-        return 0
-
-    lax.fori_loop(0, nx, score, 0)
+        push[...] += pulled(r)
+        return 0
+
+    far = nx - 1
+    lax.fori_loop(0, far, work, 0)
     back[owner] = grads[owner]
-
-    table = frows[...].reshape(owners * cap, width)
-
-    def pull(t, _):
-        rows = pl.ds(pl.multiple_of(t * tile, tile), tile)
-        emb_grad = lax.dot_general(
-            dscore[:, rows], table, (((0,), (0,)), ((), ())), preferred_element_type=F32
-        )
-        inner[rows, :] = (emb_grad * slope[rows, :]).astype(BF16)
-        return 0
-
-    lax.fori_loop(0, documents // tile, pull, 0)
+    arrived(2 * far)
+    arrived(2 * far + 1)
+    score(far)
+
+    inner[...] = ((push[...] + pulled(far)) * slope[...]).astype(BF16)
 
     def outer(which):
         side = docs[:, pl.ds(pl.multiple_of(which * half, half), half)]
@@ -228,6 +244,9 @@
     swap = remote(enc.at[1 - c], sib, s_sib, r_sib, chip(0, 0, 0, 1 - c))
     swap.start()
     outer(c)
+    row_grads(far)
+    grad_copy(2 * far).start()
+    grad_copy(2 * far + 1).start()
     swap.wait()
 
     def join_p(q, _):
@@ -278,17 +297,9 @@
 
     for n in range(1, owners):
         grad_copy(n).wait()
-    returned = back[...].reshape(owners * cap, width)
-    span = ny * depth
-
-    def gather_rows(k, _):
-        rows = pl.ds(pl.multiple_of(k * span, span), span)
-        total = jnp.dot(onehot[rows, :], returned, preferred_element_type=F32).reshape(ny, depth, width)
-        own[k] = total
-        ownb[k] = total.astype(BF16)
-        return 0
-
-    lax.fori_loop(0, nz, gather_rows, 0)
+    total = jnp.dot(onehot[...], back[...].reshape(owners * cap, width), preferred_element_type=F32)
+    own[...] = total.reshape(own.shape)
+    ownb[...] = total.astype(BF16).reshape(ownb.shape)
     first_a, first_b, second_a, second_b = [], [], [], []
     for j in cols:
         py = lax.rem(y + j, ny)
@@ -392,6 +403,7 @@
     docs, width = documents.shape
     held = label_slab.shape[0]
     owners, cap = request_ids.shape
+    picks = shortlist.shape[1]
     plane = nx * ny
     depth = held // (ny * nz)
     wide = 2 * width // 3
@@ -402,18 +414,22 @@
     f32 = lambda *shape: pltpu.VMEM(shape, F32)
     b16 = lambda *shape: pltpu.VMEM(shape, BF16)
     i32 = lambda *shape: pltpu.VMEM(shape, I32)
+    i16 = lambda *shape: pltpu.VMEM(shape, I16)
     dma = lambda n: [pltpu.SemaphoreType.DMA((n,))] * 2
     vmem = pl.BlockSpec(memory_space=pltpu.VMEM)
+    anywhere = pl.BlockSpec(memory_space=pl.ANY)
     slab_grad, enc_grad = pl.pallas_call(
         functools.partial(step_kernel, dims),
         out_shape=(jax.ShapeDtypeStruct((depth, width), F32), jax.ShapeDtypeStruct((2, half, width), F32)),
-        in_specs=[vmem] * 7 + [pl.BlockSpec(memory_space=pltpu.SMEM)],
+        in_specs=[anywhere] * 3 + [vmem] * 2 + [anywhere] * 2 + [pl.BlockSpec(memory_space=pltpu.SMEM)],
         out_specs=[vmem] * 2,
         scratch_shapes=[
-            b16(docs, width), f32(docs, width), b16(held, slot_count),
+            b16(docs, width), b16(width, width), b16(held, width), i32(picks, docs), i32(picks, docs),
+            i16(picks, docs), i16(picks, docs),
+            b16(docs, width), f32(docs, width), f32(docs, width), b16(held, slot_count),
             b16(owners, cap, width), b16(owners, cap, width),
             b16(owners, 16, cap), b16(owners, 16, cap), i32(owners, 1, cap),
-            i32(2 * cap, docs), b16(slot_count, docs),
+            i16(slot_count, docs), b16(slot_count, docs),
             b16(owners, cap, width), b16(owners, cap, width),
             f32(nz, ny, depth, width), b16(nz, ny, depth, width),
             b16(ny - 1, nz, depth, wide), b16(nz - 1, ny, depth, slim),
@@ -423,7 +439,7 @@
             b16(plane, piece, width), b16(nz, piece, width),
             b16(plane - 1, piece, width), b16(nz - 1, piece, width),
             f32(nz, piece, width), f32(plane, piece, width),
-            *dma(owners), *dma(owners), *dma(owners), *dma(owners),
+            pltpu.SemaphoreType.DMA((5,)), *dma(owners), *dma(owners), *dma(owners), *dma(owners),
             *dma(ny - 1), *dma(nz - 1), *dma(nz - 1), *dma(ny - 1),
             pltpu.SemaphoreType.DMA, pltpu.SemaphoreType.DMA,
             *dma(plane - 1), *dma(nz - 1), *dma(nz - 1), *dma(plane - 1), *dma(plane - 1), *dma(nz - 1),
@@ -438,10 +454,10 @@
         documents,
         enc_weight,
         label_slab,
-        row_scale.reshape(1, held),
+        row_scale,
         request_ids.reshape(owners, 1, cap),
         shortlist.T,
-        (1 + 64 * positive).T,
+        positive.T,
         counts,
     )
     return slab_grad, enc_grad.reshape(width, width)

time: 103 us -> 98.1 us (0.952)
  the two profiles are of different devices: /device:TPU:1 before, /device:TPU:2 now
where the time goes in v3:
time: 98.1 us; the launch traced here: 97.9 us
  Pallas kernels  92.6 us (94%)
  local copies, waits for them, and re-layouts  4.64 us (5%)
    pallas_call x1, Pallas kernels, body(): pl.pallas_call(functools.partial(step_kernel, dims), out_shape=(jax.Shape...  92.6 us
    unnamed x2, local copies, waits for them, and re-layouts  4.64 us

profile of v3, /device:TPU:2, one launch (start us, length us, event | category | flops | bytes accessed | tf_op | source)
XLA Modules:
  0.0 97.9 jit_solution(13579824275448976997)
XLA Ops:
  0.6 92.6 %classifier_step.1 = (f32[16,768]{1,0:T(8,128)}, f32[2,384,768]{2,1,0:T(8,128)}) custom-call(bf16[1024,768]{1,0:T(8,128)(2,1)} %docs_in.1, bf16[768,768]{1,0:T(8,128)(2,1)} %weight_in.1, bf16[512,768]{1,0:T(8,128)(2,1)} %slab_in.1, bf16[512]{0:T(512)(128)(2,1)} %scale.1, s32[8,1,128]{2,1,0:T(1,128)} %bitcast.7, s32[32,1024]{1,0:T(8,128)} %bitcast.5, ...), custom_call_target="tpu_custom_call" | custom-call | flops 10000000000 | bytes 10000000 | tf_op jit(solution)/shard_map/classifier_step/pallas_call | solution.py:421
  93.3 1.4 %copy.12 = f32[16,768]{1,0:T(8,128)} copy(f32[16,768]{1,0:T(8,128)} %get-tuple-element.8) | data formatting | bytes 98304
  94.7 3.2 %copy.13 = f32[768,768]{1,0:T(8,128)} copy(f32[768,768]{1,0:T(8,128)} %bitcast.4) | data formatting | bytes 4718592

commit v4 on v3

--- a/solution.py
+++ b/solution.py
@@ -51,6 +51,7 @@
     half = enc.shape[1]
     cut = nx * ny * piece
     strip = min(128, documents)
+    far = nx - 1
 
     plane = [(i, j) for i in range(nx) for j in range(ny) if (i, j) != (0, 0)]
     rings = list(range(1, nz))
@@ -138,7 +139,7 @@
             frows[owner] = rows
             fscale[owner] = sc
 
-        @pl.when(n > 0)
+        @pl.when((n > 0) & (n < 2 * far))
         def _():
             row_copy(n).start()
             scale_copy(n).start()
@@ -204,9 +205,20 @@
         rows = frows[pl.ds(first, 2)].reshape(pair, width)
         return lax.dot_general(dscore[span, :], rows, (((0,), (0,)), ((), ())), preferred_element_type=F32)
 
+    def sent(n):
+        row_copy(n).wait_send()
+        scale_copy(n).wait_send()
+
     def arrived(n):
-        row_copy(n).wait()
-        scale_copy(n).wait()
+        row_copy(n).wait_recv()
+        scale_copy(n).wait_recv()
+
+    for n in range(2, 2 * far):
+        sent(n)
+    for n in (2 * far, 2 * far + 1):
+        row_copy(n).start()
+        scale_copy(n).start()
+    sent(1)
 
     push[...] = jnp.zeros_like(push)
 
@@ -219,19 +231,16 @@
         score(r)
         row_grads(r)
 
-        @pl.when(r > 0)
-        def _():
-            grad_copy(2 * r).start()
-
-        grad_copy(2 * r + 1).start()
         push[...] += pulled(r)
         return 0
 
-    far = nx - 1
     lax.fori_loop(0, far, work, 0)
     back[owner] = grads[owner]
-    arrived(2 * far)
-    arrived(2 * far + 1)
+    for n in (2 * far, 2 * far + 1):
+        sent(n)
+        arrived(n)
+    for n in range(1, 2 * far):
+        grad_copy(n).start()
     score(far)
 
     inner[...] = ((push[...] + pulled(far)) * slope[...]).astype(BF16)
@@ -269,30 +278,6 @@
         to = lax.rem(z + k, nz)
         q1.append(remote(accq.at[to], gotq.at[k - 1], s_q.at[k - 1], r_q.at[k - 1], chip(0, 0, k, c)))
     for copy in p1 + q1:
-        copy.start()
-
-    for copy in p1:
-        copy.wait()
-    rows = pl.ds(pl.multiple_of(here * piece, piece), piece)
-    total = enc[c, rows, :] + sib[rows, :]
-    for n in range(len(plane)):
-        total += gotp[n].astype(F32)
-    allp[z] = total
-    p2, q2 = [], []
-    for k in rings:
-        p2.append(remote(allp.at[z], allp.at[z], s_p2.at[k - 1], r_p2.at[k - 1], chip(0, 0, k, c)))
-    for copy in p2:
-        copy.start()
-    for copy in q1:
-        copy.wait()
-    rows = pl.ds(pl.multiple_of(cut + z * piece, piece), piece)
-    total = enc[c, rows, :] + sib[rows, :]
-    for k in rings:
-        total += gotq[k - 1].astype(F32)
-    allq[here] = total
-    for n, (i, j) in enumerate(plane):
-        q2.append(remote(allq.at[here], allq.at[here], s_q2.at[n], r_q2.at[n], chip(i, j, 0, c)))
-    for copy in q2:
         copy.start()
 
     for n in range(1, owners):
@@ -312,6 +297,63 @@
     for copy in first_a + first_b:
         copy.start()
 
+    for copy in p1:
+        copy.wait()
+    rows = pl.ds(pl.multiple_of(here * piece, piece), piece)
+    total = enc[c, rows, :] + sib[rows, :]
+    for n in range(len(plane)):
+        total += gotp[n].astype(F32)
+    allp[z] = total
+    p2, q2 = [], []
+    for k in rings:
+        p2.append(remote(allp.at[z], allp.at[z], s_p2.at[k - 1], r_p2.at[k - 1], chip(0, 0, k, c)))
+    for copy in p2:
+        copy.start()
+    for copy in q1:
+        copy.wait()
+    rows = pl.ds(pl.multiple_of(cut + z * piece, piece), piece)
+    total = enc[c, rows, :] + sib[rows, :]
+    for k in rings:
+        total += gotq[k - 1].astype(F32)
+    allq[here] = total
+    for n, (i, j) in enumerate(plane):
+        q2.append(remote(allq.at[here], allq.at[here], s_q2.at[n], r_q2.at[n], chip(i, j, 0, c)))
+    for copy in q2:
+        copy.start()
+
+    for copy in first_a:
+        copy.wait()
+
+    def join_a(q, _):
+        total = own[q, y, :, 0:wide]
+        for j in cols:
+            total += gota[j - 1, q].astype(F32)
+        acca[q] = total
+        return 0
+
+    lax.fori_loop(0, nz, join_a, 0)
+    for k in rings:
+        pz = lax.rem(z + k, nz)
+        second_a.append(remote(acca.at[pz], gota2.at[k - 1], s_a2.at[k - 1], r_a2.at[k - 1], chip(0, 0, k, c)))
+    for copy in second_a:
+        copy.start()
+    for copy in first_b:
+        copy.wait()
+
+    def join_b(q, _):
+        total = own[z, q, :, wide:]
+        for k in rings:
+            total += gotb[k - 1, q].astype(F32)
+        accb[q] = total
+        return 0
+
+    lax.fori_loop(0, ny, join_b, 0)
+    for j in cols:
+        py = lax.rem(y + j, ny)
+        second_b.append(remote(accb.at[py], gotb2.at[j - 1], s_b2.at[j - 1], r_b2.at[j - 1], chip(0, j, 0, c)))
+    for copy in second_b:
+        copy.start()
+
     p3, q3 = [], []
     for copy in p2:
         copy.wait()
@@ -338,49 +380,20 @@
     for copy in q3:
         copy.start()
 
-    for copy in first_a:
-        copy.wait()
-
-    def join_a(q, _):
-        total = own[q, y, :, 0:wide]
-        for j in cols:
-            total += gota[j - 1, q].astype(F32)
-        acca[q] = total
-        return 0
-
-    lax.fori_loop(0, nz, join_a, 0)
-    for k in rings:
-        pz = lax.rem(z + k, nz)
-        second_a.append(remote(acca.at[pz], gota2.at[k - 1], s_a2.at[k - 1], r_a2.at[k - 1], chip(0, 0, k, c)))
-    for copy in second_a:
-        copy.start()
-    for copy in first_b:
-        copy.wait()
-
-    def join_b(q, _):
-        total = own[z, q, :, wide:]
-        for k in rings:
-            total += gotb[k - 1, q].astype(F32)
-        accb[q] = total
-        return 0
-
-    lax.fori_loop(0, ny, join_b, 0)
-    for j in cols:
-        py = lax.rem(y + j, ny)
-        second_b.append(remote(accb.at[py], gotb2.at[j - 1], s_b2.at[j - 1], r_b2.at[j - 1], chip(0, j, 0, c)))
-    for copy in second_b:
-        copy.start()
-
-    for copy in p3:
-        copy.wait()
-    upper = enc_out.at[c, 0:cut, :]
-    lower = enc_out.at[c, cut:half, :]
-    last_p = remote(upper, upper, s_e.at[0], r_e.at[0], chip(0, 0, 0, 1 - c))
-    last_p.start()
-    for copy in q3:
-        copy.wait()
-    last_q = remote(lower, lower, s_e.at[1], r_e.at[1], chip(0, 0, 0, 1 - c))
-    last_q.start()
+    def pass_on(first, n):
+        part = enc_out.at[c, pl.ds(pl.multiple_of(first, piece), piece), :]
+        copy = remote(part, part, s_e.at[n], r_e.at[n], chip(0, 0, 0, 1 - c))
+        copy.start()
+        return copy
+
+    handed = [pass_on(here * piece, 0), pass_on(cut + z * piece, 1)]
+    for k in rings:
+        q3[k - 1].wait()
+        handed.append(pass_on(cut + lax.rem(z + nz - k, nz) * piece, 1 + k))
+    for n, (i, j) in enumerate(plane):
+        p3[n].wait()
+        source = lax.rem(x + nx - i, nx) * ny + lax.rem(y + ny - j, ny)
+        handed.append(pass_on(source * piece, nz + 1 + n))
 
     for copy in second_a:
         copy.wait()
@@ -394,8 +407,32 @@
     for j in cols:
         total += gotb2[j - 1]
     slab_out[:, wide:] = total
-    last_p.wait()
-    last_q.wait()
+    for copy in handed:
+        copy.wait()
+
+
+def settle_kernel(slab, enc, slab_out, enc_out, sems):
+    rows = enc.shape[0] // 4
+    copies = [pltpu.make_async_copy(slab, slab_out, sems.at[4])]
+    for n in range(4):
+        part = pl.ds(n * rows, rows)
+        copies.append(pltpu.make_async_copy(enc.at[part], enc_out.at[part], sems.at[n]))
+    for copy in copies:
+        copy.start()
+    for copy in copies:
+        copy.wait()
+
+
+def settle(slab, enc):
+    anywhere = pl.BlockSpec(memory_space=pl.ANY)
+    return pl.pallas_call(
+        settle_kernel,
+        out_shape=(jax.ShapeDtypeStruct(slab.shape, F32), jax.ShapeDtypeStruct(enc.shape, F32)),
+        in_specs=[anywhere] * 2,
+        out_specs=[anywhere] * 2,
+        scratch_shapes=[pltpu.SemaphoreType.DMA((5,))],
+        name="settle",
+    )(slab, enc)
 
 
 def body(dims, documents, enc_weight, label_slab, row_scale, shortlist, positive, request_ids, counts):
@@ -443,7 +480,7 @@
             *dma(ny - 1), *dma(nz - 1), *dma(nz - 1), *dma(ny - 1),
             pltpu.SemaphoreType.DMA, pltpu.SemaphoreType.DMA,
             *dma(plane - 1), *dma(nz - 1), *dma(nz - 1), *dma(plane - 1), *dma(plane - 1), *dma(nz - 1),
-            *dma(2),
+            *dma(plane + nz),
         ],
         compiler_params=pltpu.CompilerParams(
             collective_id=1, has_side_effects=True, vmem_limit_bytes=56 * 2**20
@@ -460,7 +497,7 @@
         positive.T,
         counts,
     )
-    return slab_grad, enc_grad.reshape(width, width)
+    return settle(slab_grad, enc_grad.reshape(width, width))
 
 
 def solution(mesh):

time: 98.1 us -> 170 us (1.73)
  the two profiles are of different devices: /device:TPU:2 before, /device:TPU:1 now
where the time goes in v4:
time: 170 us
  Pallas kernels  170 us (100%)
    pallas_call x1, Pallas kernels, body(): pl.pallas_call(functools.partial(step_kernel, dims), out_shape=(jax.Shape...  95.6 us
    pallas_call x1, Pallas kernels, settle(): pl.pallas_call(settle_kernel, out_shape=(jax.ShapeDtypeStruct(slab.shape,...  74.1 us

profile of v4, /device:TPU:1, one launch (start us, length us, event | category | flops | bytes accessed | tf_op | source)
XLA Modules:
  0.0 170.3 jit_solution(6726316355441247996)
XLA Ops:
  0.6 95.6 %classifier_step.1 = (f32[16,768]{1,0:T(8,128)}, f32[2,384,768]{2,1,0:T(8,128)}) custom-call(bf16[1024,768]{1,0:T(8,128)(2,1)} %docs_in.1, bf16[768,768]{1,0:T(8,128)(2,1)} %weight_in.1, bf16[512,768]{1,0:T(8,128)(2,1)} %slab_in.1, bf16[512]{0:T(512)(128)(2,1)} %scale.1, s32[8,1,128]{2,1,0:T(1,128)} %bitcast.7, s32[32,1024]{1,0:T(8,128)} %bitcast.5, ...), custom_call_target="tpu_custom_call" | custom-call | flops 10000000000 | bytes 10000000 | tf_op jit(solution)/shard_map/classifier_step/pallas_call | solution.py:458
  96.2 74.1 %settle.1 = (f32[16,768]{1,0:T(8,128)}, f32[768,768]{1,0:T(8,128)}) custom-call(f32[16,768]{1,0:T(8,128)} %get-tuple-element.4.slab, f32[768,768]{1,0:T(8,128)} %bitcast.4), custom_call_target="tpu_custom_call" | custom-call | tf_op jit(solution)/shard_map/settle/pallas_call | solution.py:428

commit v5 on v4

--- a/solution.py
+++ b/solution.py
@@ -30,10 +30,10 @@
     dims, docs_in, weight_in, slab_in, scale, ids, slots_in, on_in, counts, slab_out, enc_out,
     docs, weight, slab, slots32, on32, slots, marks, emb, slope, push, onehot, srows, frows, sscale, fscale, gids, tally, dscore, grads, back,
     own, ownb, gota, gotb, acca, accb, gota2, gotb2,
-    inner, enc, sib, accp, accq, gotp, gotq, allp, allq,
+    inner, enc, sib, accp, accq, gotp, gotq, allp, allx, ally,
     s_in, s_id, r_id, s_f, r_f, s_c, r_c, s_g, r_g,
     s_a, r_a, s_b, r_b, s_a2, r_a2, s_b2, r_b2,
-    s_sib, r_sib, s_p, r_p, s_q, r_q, s_p2, r_p2, s_q2, r_q2, s_p3, r_p3, s_q3, r_q3, s_e, r_e,
+    s_sib, r_sib, s_p, r_p, s_q, r_q, s_p2, r_p2, s_x, r_x, s_y, r_y, s_p3, r_p3, s_q3, r_q3, s_e, r_e,
 ):
     nx, ny, nz = dims
     owner, group = lax.axis_index("owner"), lax.axis_index("dp")
@@ -139,7 +139,7 @@
             frows[owner] = rows
             fscale[owner] = sc
 
-        @pl.when((n > 0) & (n < 2 * far))
+        @pl.when(n > 0)
         def _():
             row_copy(n).start()
             scale_copy(n).start()
@@ -205,20 +205,9 @@
         rows = frows[pl.ds(first, 2)].reshape(pair, width)
         return lax.dot_general(dscore[span, :], rows, (((0,), (0,)), ((), ())), preferred_element_type=F32)
 
-    def sent(n):
-        row_copy(n).wait_send()
-        scale_copy(n).wait_send()
-
     def arrived(n):
-        row_copy(n).wait_recv()
-        scale_copy(n).wait_recv()
-
-    for n in range(2, 2 * far):
-        sent(n)
-    for n in (2 * far, 2 * far + 1):
-        row_copy(n).start()
-        scale_copy(n).start()
-    sent(1)
+        row_copy(n).wait()
+        scale_copy(n).wait()
 
     push[...] = jnp.zeros_like(push)
 
@@ -231,16 +220,18 @@
         score(r)
         row_grads(r)
 
+        @pl.when(r > 0)
+        def _():
+            grad_copy(2 * r).start()
+
+        grad_copy(2 * r + 1).start()
         push[...] += pulled(r)
         return 0
 
     lax.fori_loop(0, far, work, 0)
     back[owner] = grads[owner]
-    for n in (2 * far, 2 * far + 1):
-        sent(n)
-        arrived(n)
-    for n in range(1, 2 * far):
-        grad_copy(n).start()
+    arrived(2 * far)
+    arrived(2 * far + 1)
     score(far)
 
     inner[...] = ((push[...] + pulled(far)) * slope[...]).astype(BF16)
@@ -315,9 +306,9 @@
     total = enc[c, rows, :] + sib[rows, :]
     for k in rings:
         total += gotq[k - 1].astype(F32)
-    allq[here] = total
-    for n, (i, j) in enumerate(plane):
-        q2.append(remote(allq.at[here], allq.at[here], s_q2.at[n], r_q2.at[n], chip(i, j, 0, c)))
+    allx[x] = total
+    for i in range(1, nx):
+        q2.append(remote(allx.at[x], allx.at[x], s_x.at[i - 1], r_x.at[i - 1], chip(i, 0, 0, c)))
     for copy in q2:
         copy.start()
 
@@ -352,6 +343,18 @@
         py = lax.rem(y + j, ny)
         second_b.append(remote(accb.at[py], gotb2.at[j - 1], s_b2.at[j - 1], r_b2.at[j - 1], chip(0, j, 0, c)))
     for copy in second_b:
+        copy.start()
+
+    for copy in q2:
+        copy.wait()
+    total = allx[0]
+    for i in range(1, nx):
+        total += allx[i]
+    ally[y] = total
+    q2 = []
+    for j in cols:
+        q2.append(remote(ally.at[y], ally.at[y], s_y.at[j - 1], r_y.at[j - 1], chip(0, j, 0, c)))
+    for copy in q2:
         copy.start()
 
     p3, q3 = [], []
@@ -369,9 +372,9 @@
         copy.start()
     for copy in q2:
         copy.wait()
-    total = allq[0]
-    for k in range(1, nx * ny):
-        total += allq[k]
+    total = ally[0]
+    for j in cols:
+        total += ally[j]
     rows_q = pl.ds(pl.multiple_of(cut + z * piece, piece), piece)
     enc_out[c, rows_q, :] = total
     for k in rings:
@@ -428,7 +431,7 @@
     return pl.pallas_call(
         settle_kernel,
         out_shape=(jax.ShapeDtypeStruct(slab.shape, F32), jax.ShapeDtypeStruct(enc.shape, F32)),
-        in_specs=[anywhere] * 2,
+        in_specs=[pl.BlockSpec(memory_space=pltpu.VMEM)] * 2,
         out_specs=[anywhere] * 2,
         scratch_shapes=[pltpu.SemaphoreType.DMA((5,))],
         name="settle",
@@ -475,11 +478,11 @@
             b16(docs, width), f32(2, half, width), f32(half, width),
             b16(plane, piece, width), b16(nz, piece, width),
             b16(plane - 1, piece, width), b16(nz - 1, piece, width),
-            f32(nz, piece, width), f32(plane, piece, width),
+            f32(nz, piece, width), f32(nx, piece, width), f32(ny, piece, width),
             pltpu.SemaphoreType.DMA((5,)), *dma(owners), *dma(owners), *dma(owners), *dma(owners),
             *dma(ny - 1), *dma(nz - 1), *dma(nz - 1), *dma(ny - 1),
             pltpu.SemaphoreType.DMA, pltpu.SemaphoreType.DMA,
-            *dma(plane - 1), *dma(nz - 1), *dma(nz - 1), *dma(plane - 1), *dma(plane - 1), *dma(nz - 1),
+            *dma(plane - 1), *dma(nz - 1), *dma(nz - 1), *dma(nx - 1), *dma(ny - 1), *dma(plane - 1), *dma(nz - 1),
             *dma(plane + nz),
         ],
         compiler_params=pltpu.CompilerParams(

time: 170 us -> 95.5 us (0.56)
  Pallas kernels: 170 us -> 94.7 us
    pallas_call x1, Pallas kernels: 74.1 us -> 3.15 us  [settle(): pl.pallas_call(settle_kernel, out_shape=(jax.ShapeDtypeStruct(slab.shape,...]
    pallas_call x1, Pallas kernels: 95.6 us -> 91.6 us  [body(): pl.pallas_call(functools.partial(step_kernel, dims), out_shape=(jax.Shape...]
where the time goes in v5:
time: 95.5 us; the launch traced here: 95.4 us
  Pallas kernels  94.7 us (99%)
    pallas_call x1, Pallas kernels, body(): pl.pallas_call(functools.partial(step_kernel, dims), out_shape=(jax.Shape...  91.6 us
    pallas_call x1, Pallas kernels, settle(): pl.pallas_call(settle_kernel, out_shape=(jax.ShapeDtypeStruct(slab.shape,...  3.15 us

profile of v5, /device:TPU:1, one launch (start us, length us, event | category | flops | bytes accessed | tf_op | source)
XLA Modules:
  0.0 95.4 jit_solution(16339450985705963291)
XLA Ops:
  0.6 91.6 %classifier_step.1 = (f32[16,768]{1,0:T(8,128)}, f32[2,384,768]{2,1,0:T(8,128)}) custom-call(bf16[1024,768]{1,0:T(8,128)(2,1)} %docs_in.1, bf16[768,768]{1,0:T(8,128)(2,1)} %weight_in.1, bf16[512,768]{1,0:T(8,128)(2,1)} %slab_in.1, bf16[512]{0:T(512)(128)(2,1)} %scale.1, s32[8,1,128]{2,1,0:T(1,128)} %bitcast.7, s32[32,1024]{1,0:T(8,128)} %bitcast.5, ...), custom_call_target="tpu_custom_call" | custom-call | flops 10000000000 | bytes 10000000 | tf_op jit(solution)/shard_map/classifier_step/pallas_call | solution.py:461
  92.2 3.2 %settle.1 = (f32[16,768]{1,0:T(8,128)}, f32[768,768]{1,0:T(8,128)}) custom-call(f32[16,768]{1,0:T(8,128)} %get-tuple-element.4.slab, f32[768,768]{1,0:T(8,128)} %bitcast.4), custom_call_target="tpu_custom_call" | custom-call | tf_op jit(solution)/shard_map/settle/pallas_call | solution.py:431

commit v6 on v5

--- a/solution.py
+++ b/solution.py
@@ -47,7 +47,7 @@
     rows_held = slab.shape[0]
     wide = gota.shape[-1]
     depth = gota.shape[-2]
-    piece = accp.shape[1]
+    piece = accp.shape[2]
     half = enc.shape[1]
     cut = nx * ny * piece
     strip = min(128, documents)
@@ -236,180 +236,217 @@
 
     inner[...] = ((push[...] + pulled(far)) * slope[...]).astype(BF16)
 
-    def outer(which):
+    parts = range(2)
+    part_width = width // 2
+
+    def columns(h):
+        return pl.ds(h * part_width, part_width)
+
+    def outer(which, h):
         side = docs[:, pl.ds(pl.multiple_of(which * half, half), half)]
-        enc[which] = lax.dot_general(side, inner[...], (((0,), (0,)), ((), ())), preferred_element_type=F32)
-
-    outer(1 - c)
-    swap = remote(enc.at[1 - c], sib, s_sib, r_sib, chip(0, 0, 0, 1 - c))
-    swap.start()
-    outer(c)
+        enc[which, :, columns(h)] = lax.dot_general(
+            side, inner[:, columns(h)], (((0,), (0,)), ((), ())), preferred_element_type=F32
+        )
+
+    swaps = [
+        remote(enc.at[1 - c, :, columns(h)], sib.at[:, columns(h)], s_sib.at[h], r_sib.at[h], chip(0, 0, 0, 1 - c))
+        for h in parts
+    ]
+    for h in parts:
+        outer(1 - c, h)
+        swaps[h].start()
+    for h in parts:
+        outer(c, h)
     row_grads(far)
     grad_copy(2 * far).start()
     grad_copy(2 * far + 1).start()
-    swap.wait()
-
-    def join_p(q, _):
-        rows = pl.ds(pl.multiple_of(q * piece, piece), piece)
-        accp[q] = (enc[c, rows, :] + sib[rows, :]).astype(BF16)
-        return 0
-
-    def join_q(q, _):
-        rows = pl.ds(pl.multiple_of(cut + q * piece, piece), piece)
-        accq[q] = (enc[c, rows, :] + sib[rows, :]).astype(BF16)
-        return 0
-
-    lax.fori_loop(0, nx * ny, join_p, 0)
-    lax.fori_loop(0, nz, join_q, 0)
-    p1, q1 = [], []
-    for n, (i, j) in enumerate(plane):
-        to = lax.rem(x + i, nx) * ny + lax.rem(y + j, ny)
-        p1.append(remote(accp.at[to], gotp.at[n], s_p.at[n], r_p.at[n], chip(i, j, 0, c)))
-    for k in rings:
-        to = lax.rem(z + k, nz)
-        q1.append(remote(accq.at[to], gotq.at[k - 1], s_q.at[k - 1], r_q.at[k - 1], chip(0, 0, k, c)))
-    for copy in p1 + q1:
-        copy.start()
+
+    def summed(first, h):
+        rows = pl.ds(pl.multiple_of(first, piece), piece)
+        return enc[c, rows, columns(h)] + sib[rows, columns(h)]
+
+    p1, q1 = [[], []], [[], []]
+    for h in parts:
+        swaps[h].wait()
+
+        def join_p(q, _):
+            accp[h, q] = summed(q * piece, h).astype(BF16)
+            return 0
+
+        def join_q(q, _):
+            accq[h, q] = summed(cut + q * piece, h).astype(BF16)
+            return 0
+
+        lax.fori_loop(0, nx * ny, join_p, 0)
+        lax.fori_loop(0, nz, join_q, 0)
+        for n, (i, j) in enumerate(plane):
+            to = lax.rem(x + i, nx) * ny + lax.rem(y + j, ny)
+            p1[h].append(remote(accp.at[h, to], gotp.at[h, n], s_p.at[h, n], r_p.at[h, n], chip(i, j, 0, c)))
+        for k in rings:
+            to = lax.rem(z + k, nz)
+            q1[h].append(
+                remote(accq.at[h, to], gotq.at[h, k - 1], s_q.at[h, k - 1], r_q.at[h, k - 1], chip(0, 0, k, c))
+            )
+        for copy in p1[h] + q1[h]:
+            copy.start()
+
+    p2, qx, qy = [[], []], [[], []], [[], []]
+    for h in parts:
+        for copy in p1[h]:
+            copy.wait()
+        total = summed(here * piece, h)
+        for n in range(len(plane)):
+            total += gotp[h, n].astype(F32)
+        allp[h, z] = total
+        for k in rings:
+            p2[h].append(
+                remote(allp.at[h, z], allp.at[h, z], s_p2.at[h, k - 1], r_p2.at[h, k - 1], chip(0, 0, k, c))
+            )
+        for copy in p2[h]:
+            copy.start()
+        for copy in q1[h]:
+            copy.wait()
+        total = summed(cut + z * piece, h)
+        for k in rings:
+            total += gotq[h, k - 1].astype(F32)
+        allx[h, x] = total
+        for i in range(1, nx):
+            qx[h].append(remote(allx.at[h, x], allx.at[h, x], s_x.at[h, i - 1], r_x.at[h, i - 1], chip(i, 0, 0, c)))
+        for copy in qx[h]:
+            copy.start()
 
     for n in range(1, owners):
         grad_copy(n).wait()
     total = jnp.dot(onehot[...], back[...].reshape(owners * cap, width), preferred_element_type=F32)
     own[...] = total.reshape(own.shape)
     ownb[...] = total.astype(BF16).reshape(ownb.shape)
-    first_a, first_b, second_a, second_b = [], [], [], []
-    for j in cols:
-        py = lax.rem(y + j, ny)
-        first_a.append(remote(ownb.at[:, py, :, 0:wide], gota.at[j - 1], s_a.at[j - 1], r_a.at[j - 1],
-                              chip(0, j, 0, c)))
-    for k in rings:
-        pz = lax.rem(z + k, nz)
-        first_b.append(remote(ownb.at[pz, :, :, wide:], gotb.at[k - 1], s_b.at[k - 1], r_b.at[k - 1],
-                              chip(0, 0, k, c)))
-    for copy in first_a + first_b:
+
+    def cols_a(h):
+        return pl.ds(h * part_width, wide)
+
+    def cols_b(h):
+        return pl.ds(h * part_width + wide, part_width - wide)
+
+    first_a, first_b, second_a, second_b = [[], []], [[], []], [[], []], [[], []]
+    for h in parts:
+        for j in cols:
+            py = lax.rem(y + j, ny)
+            first_a[h].append(remote(ownb.at[:, py, :, cols_a(h)], gota.at[h, j - 1], s_a.at[h, j - 1],
+                                     r_a.at[h, j - 1], chip(0, j, 0, c)))
+        for k in rings:
+            pz = lax.rem(z + k, nz)
+            first_b[h].append(remote(ownb.at[pz, :, :, cols_b(h)], gotb.at[h, k - 1], s_b.at[h, k - 1],
+                                     r_b.at[h, k - 1], chip(0, 0, k, c)))
+        for copy in first_a[h] + first_b[h]:
+            copy.start()
+
+    for h in parts:
+        for copy in qx[h]:
+            copy.wait()
+        total = allx[h, 0]
+        for i in range(1, nx):
+            total += allx[h, i]
+        ally[h, y] = total
+        for j in cols:
+            qy[h].append(remote(ally.at[h, y], ally.at[h, y], s_y.at[h, j - 1], r_y.at[h, j - 1], chip(0, j, 0, c)))
+        for copy in qy[h]:
+            copy.start()
+
+    p3, q3 = [[], []], [[], []]
+    rows_p = pl.ds(pl.multiple_of(here * piece, piece), piece)
+    rows_q = pl.ds(pl.multiple_of(cut + z * piece, piece), piece)
+    for h in parts:
+        for copy in p2[h]:
+            copy.wait()
+        total = allp[h, 0]
+        for k in range(1, nz):
+            total += allp[h, k]
+        enc_out[c, rows_p, columns(h)] = total
+        part = enc_out.at[c, rows_p, columns(h)]
+        for n, (i, j) in enumerate(plane):
+            p3[h].append(remote(part, part, s_p3.at[h, n], r_p3.at[h, n], chip(i, j, 0, c)))
+        for copy in p3[h]:
+            copy.start()
+        for copy in qy[h]:
+            copy.wait()
+        total = ally[h, 0]
+        for j in cols:
+            total += ally[h, j]
+        enc_out[c, rows_q, columns(h)] = total
+        part = enc_out.at[c, rows_q, columns(h)]
+        for k in rings:
+            q3[h].append(remote(part, part, s_q3.at[h, k - 1], r_q3.at[h, k - 1], chip(0, 0, k, c)))
+        for copy in q3[h]:
+            copy.start()
+
+    for h in parts:
+        for copy in first_a[h]:
+            copy.wait()
+
+        def join_a(q, _):
+            total = own[q, y, :, cols_a(h)]
+            for j in cols:
+                total += gota[h, j - 1, q].astype(F32)
+            acca[h, q] = total
+            return 0
+
+        lax.fori_loop(0, nz, join_a, 0)
+        for k in rings:
+            pz = lax.rem(z + k, nz)
+            second_a[h].append(remote(acca.at[h, pz], gota2.at[h, k - 1], s_a2.at[h, k - 1], r_a2.at[h, k - 1],
+                                      chip(0, 0, k, c)))
+        for copy in second_a[h]:
+            copy.start()
+        for copy in first_b[h]:
+            copy.wait()
+
+        def join_b(q, _):
+            total = own[z, q, :, cols_b(h)]
+            for k in rings:
+                total += gotb[h, k - 1, q].astype(F32)
+            accb[h, q] = total
+            return 0
+
+        lax.fori_loop(0, ny, join_b, 0)
+        for j in cols:
+            py = lax.rem(y + j, ny)
+            second_b[h].append(remote(accb.at[h, py], gotb2.at[h, j - 1], s_b2.at[h, j - 1], r_b2.at[h, j - 1],
+                                      chip(0, j, 0, c)))
+        for copy in second_b[h]:
+            copy.start()
+
+    handed = []
+
+    def pass_on(first, h, n):
+        part = enc_out.at[c, pl.ds(pl.multiple_of(first, piece), piece), columns(h)]
+        copy = remote(part, part, s_e.at[h, n], r_e.at[h, n], chip(0, 0, 0, 1 - c))
         copy.start()
-
-    for copy in p1:
-        copy.wait()
-    rows = pl.ds(pl.multiple_of(here * piece, piece), piece)
-    total = enc[c, rows, :] + sib[rows, :]
-    for n in range(len(plane)):
-        total += gotp[n].astype(F32)
-    allp[z] = total
-    p2, q2 = [], []
-    for k in rings:
-        p2.append(remote(allp.at[z], allp.at[z], s_p2.at[k - 1], r_p2.at[k - 1], chip(0, 0, k, c)))
-    for copy in p2:
-        copy.start()
-    for copy in q1:
-        copy.wait()
-    rows = pl.ds(pl.multiple_of(cut + z * piece, piece), piece)
-    total = enc[c, rows, :] + sib[rows, :]
-    for k in rings:
-        total += gotq[k - 1].astype(F32)
-    allx[x] = total
-    for i in range(1, nx):
-        q2.append(remote(allx.at[x], allx.at[x], s_x.at[i - 1], r_x.at[i - 1], chip(i, 0, 0, c)))
-    for copy in q2:
-        copy.start()
-
-    for copy in first_a:
-        copy.wait()
-
-    def join_a(q, _):
-        total = own[q, y, :, 0:wide]
+        handed.append(copy)
+
+    for h in parts:
+        pass_on(here * piece, h, 0)
+        pass_on(cut + z * piece, h, 1)
+        for k in rings:
+            q3[h][k - 1].wait()
+            pass_on(cut + lax.rem(z + nz - k, nz) * piece, h, 1 + k)
+        for n, (i, j) in enumerate(plane):
+            p3[h][n].wait()
+            source = lax.rem(x + nx - i, nx) * ny + lax.rem(y + ny - j, ny)
+            pass_on(source * piece, h, nz + 1 + n)
+
+    for h in parts:
+        for copy in second_a[h]:
+            copy.wait()
+        total = acca[h, z]
+        for k in rings:
+            total += gota2[h, k - 1]
+        slab_out[:, cols_a(h)] = total
+        for copy in second_b[h]:
+            copy.wait()
+        total = accb[h, y]
         for j in cols:
-            total += gota[j - 1, q].astype(F32)
-        acca[q] = total
-        return 0
-
-    lax.fori_loop(0, nz, join_a, 0)
-    for k in rings:
-        pz = lax.rem(z + k, nz)
-        second_a.append(remote(acca.at[pz], gota2.at[k - 1], s_a2.at[k - 1], r_a2.at[k - 1], chip(0, 0, k, c)))
-    for copy in second_a:
-        copy.start()
-    for copy in first_b:
-        copy.wait()
-
-    def join_b(q, _):
-        total = own[z, q, :, wide:]
-        for k in rings:
-            total += gotb[k - 1, q].astype(F32)
-        accb[q] = total
-        return 0
-
-    lax.fori_loop(0, ny, join_b, 0)
-    for j in cols:
-        py = lax.rem(y + j, ny)
-        second_b.append(remote(accb.at[py], gotb2.at[j - 1], s_b2.at[j - 1], r_b2.at[j - 1], chip(0, j, 0, c)))
-    for copy in second_b:
-        copy.start()
-
-    for copy in q2:
-        copy.wait()
-    total = allx[0]
-    for i in range(1, nx):
-        total += allx[i]
-    ally[y] = total
-    q2 = []
-    for j in cols:
-        q2.append(remote(ally.at[y], ally.at[y], s_y.at[j - 1], r_y.at[j - 1], chip(0, j, 0, c)))
-    for copy in q2:
-        copy.start()
-
-    p3, q3 = [], []
-    for copy in p2:
-        copy.wait()
-    total = allp[0]
-    for k in range(1, nz):
-        total += allp[k]
-    rows_p = pl.ds(pl.multiple_of(here * piece, piece), piece)
-    enc_out[c, rows_p, :] = total
-    for n, (i, j) in enumerate(plane):
-        part = enc_out.at[c, rows_p, :]
-        p3.append(remote(part, part, s_p3.at[n], r_p3.at[n], chip(i, j, 0, c)))
-    for copy in p3:
-        copy.start()
-    for copy in q2:
-        copy.wait()
-    total = ally[0]
-    for j in cols:
-        total += ally[j]
-    rows_q = pl.ds(pl.multiple_of(cut + z * piece, piece), piece)
-    enc_out[c, rows_q, :] = total
-    for k in rings:
-        part = enc_out.at[c, rows_q, :]
-        q3.append(remote(part, part, s_q3.at[k - 1], r_q3.at[k - 1], chip(0, 0, k, c)))
-    for copy in q3:
-        copy.start()
-
-    def pass_on(first, n):
-        part = enc_out.at[c, pl.ds(pl.multiple_of(first, piece), piece), :]
-        copy = remote(part, part, s_e.at[n], r_e.at[n], chip(0, 0, 0, 1 - c))
-        copy.start()
-        return copy
-
-    handed = [pass_on(here * piece, 0), pass_on(cut + z * piece, 1)]
-    for k in rings:
-        q3[k - 1].wait()
-        handed.append(pass_on(cut + lax.rem(z + nz - k, nz) * piece, 1 + k))
-    for n, (i, j) in enumerate(plane):
-        p3[n].wait()
-        source = lax.rem(x + nx - i, nx) * ny + lax.rem(y + ny - j, ny)
-        handed.append(pass_on(source * piece, nz + 1 + n))
-
-    for copy in second_a:
-        copy.wait()
-    total = acca[z]
-    for k in rings:
-        total += gota2[k - 1]
-    slab_out[:, 0:wide] = total
-    for copy in second_b:
-        copy.wait()
-    total = accb[y]
-    for j in cols:
-        total += gotb2[j - 1]
-    slab_out[:, wide:] = total
+            total += gotb2[h, j - 1]
+        slab_out[:, cols_b(h)] = total
     for copy in handed:
         copy.wait()
 
@@ -446,8 +483,9 @@
     picks = shortlist.shape[1]
     plane = nx * ny
     depth = held // (ny * nz)
-    wide = 2 * width // 3
-    slim = width - wide
+    part = width // 2
+    wide = 2 * part // 3
+    slim = part - wide
     half = width // 2
     piece = half // (plane + nz)
     slot_count = owners * cap
@@ -456,6 +494,7 @@
     i32 = lambda *shape: pltpu.VMEM(shape, I32)
     i16 = lambda *shape: pltpu.VMEM(shape, I16)
     dma = lambda n: [pltpu.SemaphoreType.DMA((n,))] * 2
+    two = lambda n: [pltpu.SemaphoreType.DMA((2, n))] * 2
     vmem = pl.BlockSpec(memory_space=pltpu.VMEM)
     anywhere = pl.BlockSpec(memory_space=pl.ANY)
     slab_grad, enc_grad = pl.pallas_call(
@@ -472,18 +511,17 @@
             i16(slot_count, docs), b16(slot_count, docs),
             b16(owners, cap, width), b16(owners, cap, width),
             f32(nz, ny, depth, width), b16(nz, ny, depth, width),
-            b16(ny - 1, nz, depth, wide), b16(nz - 1, ny, depth, slim),
-            f32(nz, depth, wide), f32(ny, depth, slim),
-            f32(nz - 1, depth, wide), f32(ny - 1, depth, slim),
+            b16(2, ny - 1, nz, depth, wide), b16(2, nz - 1, ny, depth, slim),
+            f32(2, nz, depth, wide), f32(2, ny, depth, slim),
+            f32(2, nz - 1, depth, wide), f32(2, ny - 1, depth, slim),
             b16(docs, width), f32(2, half, width), f32(half, width),
-            b16(plane, piece, width), b16(nz, piece, width),
-            b16(plane - 1, piece, width), b16(nz - 1, piece, width),
-            f32(nz, piece, width), f32(nx, piece, width), f32(ny, piece, width),
+            b16(2, plane, piece, part), b16(2, nz, piece, part),
+            b16(2, plane - 1, piece, part), b16(2, nz - 1, piece, part),
+            f32(2, nz, piece, part), f32(2, nx, piece, part), f32(2, ny, piece, part),
             pltpu.SemaphoreType.DMA((5,)), *dma(owners), *dma(owners), *dma(owners), *dma(owners),
-            *dma(ny - 1), *dma(nz - 1), *dma(nz - 1), *dma(ny - 1),
-            pltpu.SemaphoreType.DMA, pltpu.SemaphoreType.DMA,
-            *dma(plane - 1), *dma(nz - 1), *dma(nz - 1), *dma(nx - 1), *dma(ny - 1), *dma(plane - 1), *dma(nz - 1),
-            *dma(plane + nz),
+            *two(ny - 1), *two(nz - 1), *two(nz - 1), *two(ny - 1), *dma(2),
+            *two(plane - 1), *two(nz - 1), *two(nz - 1), *two(nx - 1), *two(ny - 1), *two(plane - 1), *two(nz - 1),
+            *two(plane + nz),
         ],
         compiler_params=pltpu.CompilerParams(
             collective_id=1, has_side_effects=True, vmem_limit_bytes=56 * 2**20

time: 95.5 us -> 96.5 us (1.010)
  the two profiles are of different devices: /device:TPU:1 before, /device:TPU:2 now
where the time goes in v6:
time: 96.5 us; the launch traced here: 96.3 us
  Pallas kernels  95.7 us (99%)
    pallas_call x1, Pallas kernels, body(): pl.pallas_call(functools.partial(step_kernel, dims), out_shape=(jax.Shape...  92.5 us
    pallas_call x1, Pallas kernels, settle(): pl.pallas_call(settle_kernel, out_shape=(jax.ShapeDtypeStruct(slab.shape,...  3.15 us

profile of v6, /device:TPU:2, one launch (start us, length us, event | category | flops | bytes accessed | tf_op | source)
XLA Modules:
  0.0 96.3 jit_solution(13862494780328573777)
XLA Ops:
  0.6 92.5 %classifier_step.1 = (f32[16,768]{1,0:T(8,128)}, f32[2,384,768]{2,1,0:T(8,128)}) custom-call(bf16[1024,768]{1,0:T(8,128)(2,1)} %docs_in.1, bf16[768,768]{1,0:T(8,128)(2,1)} %weight_in.1, bf16[512,768]{1,0:T(8,128)(2,1)} %slab_in.1, bf16[512]{0:T(512)(128)(2,1)} %scale.1, s32[8,1,128]{2,1,0:T(1,128)} %bitcast.7, s32[32,1024]{1,0:T(8,128)} %bitcast.5, ...), custom_call_target="tpu_custom_call" | custom-call | flops 10000000000 | bytes 10000000 | tf_op jit(solution)/shard_map/classifier_step/pallas_call | solution.py:500
  93.2 3.2 %settle.1 = (f32[16,768]{1,0:T(8,128)}, f32[768,768]{1,0:T(8,128)}) custom-call(f32[16,768]{1,0:T(8,128)} %get-tuple-element.4.slab, f32[768,768]{1,0:T(8,128)} %bitcast.4), custom_call_target="tpu_custom_call" | custom-call | tf_op jit(solution)/shard_map/settle/pallas_call | solution.py:468

commit v7 on v3

--- a/solution.py
+++ b/solution.py
@@ -30,10 +30,10 @@
     dims, docs_in, weight_in, slab_in, scale, ids, slots_in, on_in, counts, slab_out, enc_out,
     docs, weight, slab, slots32, on32, slots, marks, emb, slope, push, onehot, srows, frows, sscale, fscale, gids, tally, dscore, grads, back,
     own, ownb, gota, gotb, acca, accb, gota2, gotb2,
-    inner, enc, sib, accp, accq, gotp, gotq, allp, allq,
+    inner, enc, sib, accp, accq, gotp, gotq, shares, gots, done, allx, ally,
     s_in, s_id, r_id, s_f, r_f, s_c, r_c, s_g, r_g,
     s_a, r_a, s_b, r_b, s_a2, r_a2, s_b2, r_b2,
-    s_sib, r_sib, s_p, r_p, s_q, r_q, s_p2, r_p2, s_q2, r_q2, s_p3, r_p3, s_q3, r_q3, s_e, r_e,
+    s_sib, r_sib, s_p, r_p, s_q, r_q, s_p2, r_p2, s_ag, r_ag, s_x, r_x, s_y, r_y, s_p3, r_p3, s_q3, r_q3, s_e, r_e,
 ):
     nx, ny, nz = dims
     owner, group = lax.axis_index("owner"), lax.axis_index("dp")
@@ -48,9 +48,11 @@
     wide = gota.shape[-1]
     depth = gota.shape[-2]
     piece = accp.shape[1]
+    share = shares.shape[1]
     half = enc.shape[1]
     cut = nx * ny * piece
     strip = min(128, documents)
+    far = nx - 1
 
     plane = [(i, j) for i in range(nx) for j in range(ny) if (i, j) != (0, 0)]
     rings = list(range(1, nz))
@@ -227,7 +229,6 @@
         push[...] += pulled(r)
         return 0
 
-    far = nx - 1
     lax.fori_loop(0, far, work, 0)
     back[owner] = grads[owner]
     arrived(2 * far)
@@ -277,10 +278,12 @@
     total = enc[c, rows, :] + sib[rows, :]
     for n in range(len(plane)):
         total += gotp[n].astype(F32)
-    allp[z] = total
+    for k in range(nz):
+        shares[k] = total[k * share : (k + 1) * share, :]
     p2, q2 = [], []
     for k in rings:
-        p2.append(remote(allp.at[z], allp.at[z], s_p2.at[k - 1], r_p2.at[k - 1], chip(0, 0, k, c)))
+        pz = lax.rem(z + k, nz)
+        p2.append(remote(shares.at[pz], gots.at[k - 1], s_p2.at[k - 1], r_p2.at[k - 1], chip(0, 0, k, c)))
     for copy in p2:
         copy.start()
     for copy in q1:
@@ -289,9 +292,9 @@
     total = enc[c, rows, :] + sib[rows, :]
     for k in rings:
         total += gotq[k - 1].astype(F32)
-    allq[here] = total
-    for n, (i, j) in enumerate(plane):
-        q2.append(remote(allq.at[here], allq.at[here], s_q2.at[n], r_q2.at[n], chip(i, j, 0, c)))
+    allx[x] = total
+    for i in range(1, nx):
+        q2.append(remote(allx.at[x], allx.at[x], s_x.at[i - 1], r_x.at[i - 1], chip(i, 0, 0, c)))
     for copy in q2:
         copy.start()
 
@@ -312,14 +315,34 @@
     for copy in first_a + first_b:
         copy.start()
 
+    for copy in p2:
+        copy.wait()
+    total = shares[z]
+    for k in rings:
+        total += gots[k - 1]
+    done[z] = total
+    p2 = []
+    for k in rings:
+        p2.append(remote(done.at[z], done.at[z], s_ag.at[k - 1], r_ag.at[k - 1], chip(0, 0, k, c)))
+    for copy in p2:
+        copy.start()
+    for copy in q2:
+        copy.wait()
+    total = allx[0]
+    for i in range(1, nx):
+        total += allx[i]
+    ally[y] = total
+    q2 = []
+    for j in cols:
+        q2.append(remote(ally.at[y], ally.at[y], s_y.at[j - 1], r_y.at[j - 1], chip(0, j, 0, c)))
+    for copy in q2:
+        copy.start()
+
     p3, q3 = [], []
     for copy in p2:
         copy.wait()
-    total = allp[0]
-    for k in range(1, nz):
-        total += allp[k]
     rows_p = pl.ds(pl.multiple_of(here * piece, piece), piece)
-    enc_out[c, rows_p, :] = total
+    enc_out[c, rows_p, :] = jnp.concatenate([done[k] for k in range(nz)], axis=0)
     for n, (i, j) in enumerate(plane):
         part = enc_out.at[c, rows_p, :]
         p3.append(remote(part, part, s_p3.at[n], r_p3.at[n], chip(i, j, 0, c)))
@@ -327,9 +350,9 @@
         copy.start()
     for copy in q2:
         copy.wait()
-    total = allq[0]
-    for k in range(1, nx * ny):
-        total += allq[k]
+    total = ally[0]
+    for j in cols:
+        total += ally[j]
     rows_q = pl.ds(pl.multiple_of(cut + z * piece, piece), piece)
     enc_out[c, rows_q, :] = total
     for k in rings:
@@ -371,16 +394,20 @@
     for copy in second_b:
         copy.start()
 
-    for copy in p3:
-        copy.wait()
-    upper = enc_out.at[c, 0:cut, :]
-    lower = enc_out.at[c, cut:half, :]
-    last_p = remote(upper, upper, s_e.at[0], r_e.at[0], chip(0, 0, 0, 1 - c))
-    last_p.start()
-    for copy in q3:
-        copy.wait()
-    last_q = remote(lower, lower, s_e.at[1], r_e.at[1], chip(0, 0, 0, 1 - c))
-    last_q.start()
+    def pass_on(first, n):
+        part = enc_out.at[c, pl.ds(pl.multiple_of(first, piece), piece), :]
+        copy = remote(part, part, s_e.at[n], r_e.at[n], chip(0, 0, 0, 1 - c))
+        copy.start()
+        return copy
+
+    handed = [pass_on(here * piece, 0), pass_on(cut + z * piece, 1)]
+    for k in rings:
+        q3[k - 1].wait()
+        handed.append(pass_on(cut + lax.rem(z + nz - k, nz) * piece, 1 + k))
+    for n, (i, j) in enumerate(plane):
+        p3[n].wait()
+        source = lax.rem(x + nx - i, nx) * ny + lax.rem(y + ny - j, ny)
+        handed.append(pass_on(source * piece, nz + 1 + n))
 
     for copy in second_a:
         copy.wait()
@@ -394,8 +421,8 @@
     for j in cols:
         total += gotb2[j - 1]
     slab_out[:, wide:] = total
-    last_p.wait()
-    last_q.wait()
+    for copy in handed:
+        copy.wait()
 
 
 def body(dims, documents, enc_weight, label_slab, row_scale, shortlist, positive, request_ids, counts):
@@ -410,6 +437,7 @@
     slim = width - wide
     half = width // 2
     piece = half // (plane + nz)
+    share = piece // nz
     slot_count = owners * cap
     f32 = lambda *shape: pltpu.VMEM(shape, F32)
     b16 = lambda *shape: pltpu.VMEM(shape, BF16)
@@ -438,15 +466,16 @@
             b16(docs, width), f32(2, half, width), f32(half, width),
             b16(plane, piece, width), b16(nz, piece, width),
             b16(plane - 1, piece, width), b16(nz - 1, piece, width),
-            f32(nz, piece, width), f32(plane, piece, width),
+            f32(nz, share, width), f32(nz - 1, share, width), f32(nz, share, width),
+            f32(nx, piece, width), f32(ny, piece, width),
             pltpu.SemaphoreType.DMA((5,)), *dma(owners), *dma(owners), *dma(owners), *dma(owners),
             *dma(ny - 1), *dma(nz - 1), *dma(nz - 1), *dma(ny - 1),
             pltpu.SemaphoreType.DMA, pltpu.SemaphoreType.DMA,
-            *dma(plane - 1), *dma(nz - 1), *dma(nz - 1), *dma(plane - 1), *dma(plane - 1), *dma(nz - 1),
-            *dma(2),
+            *dma(plane - 1), *dma(nz - 1), *dma(nz - 1), *dma(nz - 1), *dma(nx - 1), *dma(ny - 1), *dma(plane - 1), *dma(nz - 1),
+            *dma(plane + nz),
         ],
         compiler_params=pltpu.CompilerParams(
-            collective_id=1, has_side_effects=True, vmem_limit_bytes=56 * 2**20
+            collective_id=1, has_side_effects=True, vmem_limit_bytes=44 * 2**20
         ),
         cost_estimate=pl.CostEstimate(flops=10**10, bytes_accessed=10**7, transcendentals=2 * 10**6),
         name="classifier_step",

time: 98.1 us -> 97.8 us (level)
  the two profiles are of different devices: /device:TPU:2 before, /device:TPU:1 now
where the time goes in v7:
time: 97.8 us; the launch traced here: 96.9 us
  Pallas kernels  86.6 us (89%)
  local copies, waits for them, and re-layouts  9.66 us (10%)
    pallas_call x1, Pallas kernels, body(): pl.pallas_call(functools.partial(step_kernel, dims), out_shape=(jax.Shape...  86.6 us
    unnamed x18, local copies, waits for them, and re-layouts  9.66 us

profile of v7, /device:TPU:1, one launch (start us, length us, event | category | flops | bytes accessed | tf_op | source)
XLA Modules:
  0.0 96.9 jit_solution(11268625147856669165)
XLA Ops:
  0.6 0.0 copy-start
  0.6 1.4 %copy-done = bf16[1024,768]{1,0:T(8,128)(2,1)S(1)} copy-done((bf16[1024,768]{1,0:T(8,128)(2,1)S(1)}, bf16[1024,768]{1,0:T(8,128)(2,1)}, u32[]{:S(2)}) %copy-start) | copy-done | bytes 1572888
  2.0 0.0 copy-start.1
  2.0 1.3 %copy-done.1 = bf16[768,768]{1,0:T(8,128)(2,1)S(1)} copy-done((bf16[768,768]{1,0:T(8,128)(2,1)S(1)}, bf16[768,768]{1,0:T(8,128)(2,1)}, u32[]{:S(2)}) %copy-start.1) | copy-done | bytes 1179672
  3.3 0.0 copy-start.2
  3.3 1.1 %copy-done.2 = bf16[512,768]{1,0:T(8,128)(2,1)S(1)} copy-done((bf16[512,768]{1,0:T(8,128)(2,1)S(1)}, bf16[512,768]{1,0:T(8,128)(2,1)}, u32[]{:S(2)}) %copy-start.2) | copy-done | bytes 786456
  4.4 0.0 copy-start.3
  4.4 0.9 copy-done.3
  5.4 0.0 copy-start.4
  5.4 0.9 copy-done.4
  6.3 0.0 copy-start.5
  6.3 0.7 copy-done.5
  6.9 0.0 copy-start.6
  6.9 0.7 copy-done.6
  7.6 0.0 copy-start.7
  7.6 0.7 copy-done.7
  8.3 86.6 %classifier_step.1 = (f32[16,768]{1,0:T(8,128)S(1)}, f32[2,384,768]{2,1,0:T(8,128)S(1)}) custom-call(bf16[1024,768]{1,0:T(8,128)(2,1)S(1)} %copy-done, bf16[768,768]{1,0:T(8,128)(2,1)S(1)} %copy-done.1, bf16[512,768]{1,0:T(8,128)(2,1)S(1)} %copy-done.2, bf16[512]{0:T(512)(128)(2,1)S(1)} %copy-done.6, s32[8,1,128]{2,1,0:T(1,128)S(1)} %bitcast.7, ...), custom_call_target="tpu_custom_call" | custom-call | flops 10000000000 | bytes 10000000 | tf_op jit(solution)/shard_map/classifier_step/pallas_call | solution.py:449
  94.9 0.6 copy.12
  95.5 1.4 %copy.13 = f32[768,768]{1,0:T(8,128)} copy(f32[768,768]{1,0:T(8,128)S(1)} %bitcast.4) | data formatting | bytes 4718592
Async XLA Ops:
  0.6 1.4 %copy-start = (bf16[1024,768]{1,0:T(8,128)(2,1)S(1)}, bf16[1024,768]{1,0:T(8,128)(2,1)}, u32[]{:S(2)}) copy-start(bf16[1024,768]{1,0:T(8,128)(2,1)} %docs_in.1) | copy-start | bytes 4718596
  2.0 1.3 %copy-start.1 = (bf16[768,768]{1,0:T(8,128)(2,1)S(1)}, bf16[768,768]{1,0:T(8,128)(2,1)}, u32[]{:S(2)}) copy-start(bf16[768,768]{1,0:T(8,128)(2,1)} %weight_in.1) | copy-start | bytes 3538948
  3.3 1.1 %copy-start.2 = (bf16[512,768]{1,0:T(8,128)(2,1)S(1)}, bf16[512,768]{1,0:T(8,128)(2,1)}, u32[]{:S(2)}) copy-start(bf16[512,768]{1,0:T(8,128)(2,1)} %slab_in.1) | copy-start | bytes 2359300
  4.4 0.9 copy-start.3
  5.4 0.9 copy-start.4
  6.3 0.7 copy-start.5
  6.9 0.7 copy-start.6
  7.6 0.7 copy-start.7

commit v8 on v7

--- a/solution.py
+++ b/solution.py
@@ -27,8 +27,8 @@
 
 
 def step_kernel(
-    dims, docs_in, weight_in, slab_in, scale, ids, slots_in, on_in, counts, slab_out, enc_out,
-    docs, weight, slab, slots32, on32, slots, marks, emb, slope, push, onehot, srows, frows, sscale, fscale, gids, tally, dscore, grads, back,
+    dims, docs_in, weight_in, slab_in, scale_in, ids_in, slots_in, on_in, counts_in, slab_out, enc_out,
+    ids, counts, scale, docs, weight, slab, slots32, on32, slots, marks, emb, slope, push, onehot, srows, frows, sscale, fscale, gids, tally, dscore, grads, back,
     own, ownb, gota, gotb, acca, accb, gota2, gotb2,
     inner, enc, sib, accp, accq, gotp, gotq, shares, gots, done, allx, ally,
     s_in, s_id, r_id, s_f, r_f, s_c, r_c, s_g, r_g,
@@ -67,10 +67,13 @@
     loads = [
         pltpu.make_async_copy(src, dst, s_in.at[n])
         for n, (src, dst) in enumerate(
-            ((docs_in, docs), (weight_in, weight), (slab_in, slab), (slots_in, slots32), (on_in, on32))
+            (
+                (docs_in, docs), (weight_in, weight), (slab_in, slab), (slots_in, slots32), (on_in, on32),
+                (ids_in, ids), (counts_in, counts), (scale_in, scale),
+            )
         )
     ]
-    for load in loads:
+    for load in loads[5:] + loads[:5]:
         load.start()
 
     bar = pltpu.get_barrier_semaphore()
@@ -97,6 +100,7 @@
         to, _ = peer(n)
         return remote(ids.at[to], gids.at[owner], s_id.at[n], r_id.at[n], {"owner": to, "dp": group})
 
+    loads[5].wait()
     for n in range(1, owners):
         id_copy(n).start()
     gids[owner] = ids[owner]
@@ -107,6 +111,8 @@
     emb[...] = (docs[...].astype(F32) + squashed).astype(BF16)
     slope[...] = 1.0 - squashed * squashed
     loads[2].wait()
+    loads[6].wait()
+    loads[7].wait()
 
     def row_copy(n):
         to, _ = peer(n)
@@ -184,7 +190,9 @@
         for q in range(2):
             line = fscale[first + q].astype(F32)[0:1]
             factor.append(jnp.broadcast_to(line, (cap, cap)).T[:, 0:1])
-            live.append(jnp.where(lax.broadcasted_iota(I32, (cap, 1), 0) < counts[0, first + q], 1.0, 0.0))
+            lane = lax.broadcasted_iota(I32, (1, owners), 1)
+            asked = jnp.sum(jnp.where(lane == first + q, counts[...].astype(F32), 0.0), axis=1, keepdims=True)
+            live.append(jnp.where(lax.broadcasted_iota(I32, (cap, 1), 0).astype(F32) < asked, 1.0, 0.0))
         factor = jnp.concatenate(factor, axis=0)
         live = jnp.concatenate(live, axis=0)
         logits = lax.dot_general(rows, emb[...], (((1,), (1,)), ((), ())), preferred_element_type=F32) * factor
@@ -445,14 +453,13 @@
     i16 = lambda *shape: pltpu.VMEM(shape, I16)
     dma = lambda n: [pltpu.SemaphoreType.DMA((n,))] * 2
     vmem = pl.BlockSpec(memory_space=pltpu.VMEM)
-    anywhere = pl.BlockSpec(memory_space=pl.ANY)
     slab_grad, enc_grad = pl.pallas_call(
         functools.partial(step_kernel, dims),
         out_shape=(jax.ShapeDtypeStruct((depth, width), F32), jax.ShapeDtypeStruct((2, half, width), F32)),
-        in_specs=[anywhere] * 3 + [vmem] * 2 + [anywhere] * 2 + [pl.BlockSpec(memory_space=pltpu.SMEM)],
+        in_specs=[pl.BlockSpec(memory_space=pltpu.HBM)] * 8,
         out_specs=[vmem] * 2,
         scratch_shapes=[
-            b16(docs, width), b16(width, width), b16(held, width), i32(picks, docs), i32(picks, docs),
+            i32(owners, 1, cap), i32(1, owners), b16(held), b16(docs, width), b16(width, width), b16(held, width), i32(picks, docs), i32(picks, docs),
             i16(picks, docs), i16(picks, docs),
             b16(docs, width), f32(docs, width), f32(docs, width), b16(held, slot_count),
             b16(owners, cap, width), b16(owners, cap, width),
@@ -468,7 +475,7 @@
             b16(plane - 1, piece, width), b16(nz - 1, piece, width),
             f32(nz, share, width), f32(nz - 1, share, width), f32(nz, share, width),
             f32(nx, piece, width), f32(ny, piece, width),
-            pltpu.SemaphoreType.DMA((5,)), *dma(owners), *dma(owners), *dma(owners), *dma(owners),
+            pltpu.SemaphoreType.DMA((8,)), *dma(owners), *dma(owners), *dma(owners), *dma(owners),
             *dma(ny - 1), *dma(nz - 1), *dma(nz - 1), *dma(ny - 1),
             pltpu.SemaphoreType.DMA, pltpu.SemaphoreType.DMA,
             *dma(plane - 1), *dma(nz - 1), *dma(nz - 1), *dma(nz - 1), *dma(nx - 1), *dma(ny - 1), *dma(plane - 1), *dma(nz - 1),
@@ -479,7 +486,7 @@
         ),
         cost_estimate=pl.CostEstimate(flops=10**10, bytes_accessed=10**7, transcendentals=2 * 10**6),
         name="classifier_step",
-    )(
+    )(*(pltpu.with_memory_space_constraint(operand, pltpu.HBM) for operand in (
         documents,
         enc_weight,
         label_slab,
@@ -488,7 +495,7 @@
         shortlist.T,
         positive.T,
         counts,
-    )
+    )))
     return slab_grad, enc_grad.reshape(width, width)
 
 

time: 97.8 us -> 88.9 us (0.909)
  local copies, waits for them, and re-layouts: 9.66 us -> 2.03 us
  Pallas kernels: 86.6 us -> 85.4 us
    unnamed x18 -> x2, local copies, waits for them, and re-layouts: 9.66 us -> 2.03 us
    pallas_call x1, Pallas kernels: 86.6 us -> 85.4 us  [body(): pl.pallas_call(functools.partial(step_kernel, dims), out_shape=(jax.Shape...]
where the time goes in v8:
time: 88.9 us; the launch traced here: 88.1 us
  Pallas kernels  85.4 us (96%)
  local copies, waits for them, and re-layouts  2.03 us (2%)
    pallas_call x1, Pallas kernels, body(): pl.pallas_call(functools.partial(step_kernel, dims), out_shape=(jax.Shape...  85.4 us
    unnamed x2, local copies, waits for them, and re-layouts  2.03 us

profile of v8, /device:TPU:1, one launch (start us, length us, event | category | flops | bytes accessed | tf_op | source)
XLA Modules:
  0.0 88.1 jit_solution(16748331792825762494)
XLA Ops:
  0.6 85.4 %classifier_step.1 = (f32[16,768]{1,0:T(8,128)S(1)}, f32[2,384,768]{2,1,0:T(8,128)S(1)}) custom-call(bf16[1024,768]{1,0:T(8,128)(2,1)} %docs_in.1, bf16[768,768]{1,0:T(8,128)(2,1)} %weight_in.1, bf16[512,768]{1,0:T(8,128)(2,1)} %slab_in.1, bf16[512]{0:T(512)(128)(2,1)} %scale_in.1, s32[8,1,128]{2,1,0:T(1,128)} %bitcast.7, s32[32,1024]{1,0:T(8,128)} %bitcast.5, ...), custom_call_target="tpu_custom_call" | custom-call | flops 10000000000 | bytes 10000000 | tf_op jit(solution)/shard_map/classifier_step/pallas_call | solution.py:456
  86.1 0.6 copy.12
  86.7 1.4 %copy.13 = f32[768,768]{1,0:T(8,128)} copy(f32[768,768]{1,0:T(8,128)S(1)} %bitcast.4) | data formatting | bytes 4718592

commit v9 on v8

--- a/solution.py
+++ b/solution.py
@@ -157,9 +157,14 @@
         id_copy(n).wait_recv()
     lax.fori_loop(0, owners, serve, 0)
 
-    def grad_copy(n):
+    parts = range(2)
+    part_width = width // 2
+
+    def grad_copy(h, n):
         _, source = peer(n)
-        return remote(grads.at[source], back.at[owner], s_g.at[n], r_g.at[n], {"owner": source, "dp": group})
+        return remote(
+            grads.at[h, source], back.at[h, owner], s_g.at[h, n], r_g.at[h, n], {"owner": source, "dp": group}
+        )
 
     loads[3].wait()
     loads[4].wait()
@@ -205,9 +210,9 @@
 
     def row_grads(r):
         first, span = group_of(r)
-        grads[pl.ds(first, 2)] = (
-            jnp.dot(dscore[span, :], emb[...], preferred_element_type=F32).astype(BF16).reshape(2, cap, width)
-        )
+        product = jnp.dot(dscore[span, :], emb[...], preferred_element_type=F32).astype(BF16)
+        for h in parts:
+            grads[h, pl.ds(first, 2)] = product[:, h * part_width : (h + 1) * part_width].reshape(2, cap, part_width)
 
     def pulled(r):
         first, span = group_of(r)
@@ -231,17 +236,21 @@
 
         @pl.when(r > 0)
         def _():
-            grad_copy(2 * r).start()
-
-        grad_copy(2 * r + 1).start()
+            grad_copy(0, 2 * r).start()
+
+        grad_copy(0, 2 * r + 1).start()
         push[...] += pulled(r)
         return 0
 
     lax.fori_loop(0, far, work, 0)
-    back[owner] = grads[owner]
+    for h in parts:
+        back[h, owner] = grads[h, owner]
     arrived(2 * far)
     arrived(2 * far + 1)
     score(far)
+    row_grads(far)
+    grad_copy(0, 2 * far).start()
+    grad_copy(0, 2 * far + 1).start()
 
     inner[...] = ((push[...] + pulled(far)) * slope[...]).astype(BF16)
 
@@ -253,9 +262,6 @@
     swap = remote(enc.at[1 - c], sib, s_sib, r_sib, chip(0, 0, 0, 1 - c))
     swap.start()
     outer(c)
-    row_grads(far)
-    grad_copy(2 * far).start()
-    grad_copy(2 * far + 1).start()
     swap.wait()
 
     def join_p(q, _):
@@ -279,6 +285,87 @@
         q1.append(remote(accq.at[to], gotq.at[k - 1], s_q.at[k - 1], r_q.at[k - 1], chip(0, 0, k, c)))
     for copy in p1 + q1:
         copy.start()
+
+    for n in range(1, owners):
+        grad_copy(1, n).start()
+
+    def cols_a(h):
+        return pl.ds(h * part_width, wide)
+
+    def cols_b(h):
+        return pl.ds(h * part_width + wide, part_width - wide)
+
+    first_a, first_b, second_a, second_b = [[], []], [[], []], [[], []], [[], []]
+
+    def sum_rows(h):
+        for n in range(1, owners):
+            grad_copy(h, n).wait()
+        total = jnp.dot(onehot[...], back[h].reshape(owners * cap, part_width), preferred_element_type=F32)
+        here_cols = pl.ds(h * part_width, part_width)
+        own[:, :, :, here_cols] = total.reshape(nz, ny, depth, part_width)
+        ownb[:, :, :, here_cols] = total.astype(BF16).reshape(nz, ny, depth, part_width)
+        for j in cols:
+            py = lax.rem(y + j, ny)
+            first_a[h].append(remote(ownb.at[:, py, :, cols_a(h)], gota.at[h, j - 1], s_a.at[h, j - 1],
+                                     r_a.at[h, j - 1], chip(0, j, 0, c)))
+        for k in rings:
+            pz = lax.rem(z + k, nz)
+            first_b[h].append(remote(ownb.at[pz, :, :, cols_b(h)], gotb.at[h, k - 1], s_b.at[h, k - 1],
+                                     r_b.at[h, k - 1], chip(0, 0, k, c)))
+        for copy in first_a[h] + first_b[h]:
+            copy.start()
+
+    def second_rows(h):
+        for copy in first_a[h]:
+            copy.wait()
+
+        def join_a(q, _):
+            total = own[q, y, :, cols_a(h)]
+            for j in cols:
+                total += gota[h, j - 1, q].astype(F32)
+            acca[h, q] = total
+            return 0
+
+        lax.fori_loop(0, nz, join_a, 0)
+        for k in rings:
+            pz = lax.rem(z + k, nz)
+            second_a[h].append(remote(acca.at[h, pz], gota2.at[h, k - 1], s_a2.at[h, k - 1], r_a2.at[h, k - 1],
+                                      chip(0, 0, k, c)))
+        for copy in second_a[h]:
+            copy.start()
+        for copy in first_b[h]:
+            copy.wait()
+
+        def join_b(q, _):
+            total = own[z, q, :, cols_b(h)]
+            for k in rings:
+                total += gotb[h, k - 1, q].astype(F32)
+            accb[h, q] = total
+            return 0
+
+        lax.fori_loop(0, ny, join_b, 0)
+        for j in cols:
+            py = lax.rem(y + j, ny)
+            second_b[h].append(remote(accb.at[h, py], gotb2.at[h, j - 1], s_b2.at[h, j - 1], r_b2.at[h, j - 1],
+                                      chip(0, j, 0, c)))
+        for copy in second_b[h]:
+            copy.start()
+
+    def finish_rows(h):
+        for copy in second_a[h]:
+            copy.wait()
+        total = acca[h, z]
+        for k in rings:
+            total += gota2[h, k - 1]
+        slab_out[:, cols_a(h)] = total
+        for copy in second_b[h]:
+            copy.wait()
+        total = accb[h, y]
+        for j in cols:
+            total += gotb2[h, j - 1]
+        slab_out[:, cols_b(h)] = total
+
+    sum_rows(0)
 
     for copy in p1:
         copy.wait()
@@ -306,23 +393,7 @@
     for copy in q2:
         copy.start()
 
-    for n in range(1, owners):
-        grad_copy(n).wait()
-    total = jnp.dot(onehot[...], back[...].reshape(owners * cap, width), preferred_element_type=F32)
-    own[...] = total.reshape(own.shape)
-    ownb[...] = total.astype(BF16).reshape(ownb.shape)
-    first_a, first_b, second_a, second_b = [], [], [], []
-    for j in cols:
-        py = lax.rem(y + j, ny)
-        first_a.append(remote(ownb.at[:, py, :, 0:wide], gota.at[j - 1], s_a.at[j - 1], r_a.at[j - 1],
-                              chip(0, j, 0, c)))
-    for k in rings:
-        pz = lax.rem(z + k, nz)
-        first_b.append(remote(ownb.at[pz, :, :, wide:], gotb.at[k - 1], s_b.at[k - 1], r_b.at[k - 1],
-                              chip(0, 0, k, c)))
-    for copy in first_a + first_b:
-        copy.start()
-
+    second_rows(0)
     for copy in p2:
         copy.wait()
     total = shares[z]
@@ -346,6 +417,8 @@
     for copy in q2:
         copy.start()
 
+    sum_rows(1)
+
     p3, q3 = [], []
     for copy in p2:
         copy.wait()
@@ -369,38 +442,8 @@
     for copy in q3:
         copy.start()
 
-    for copy in first_a:
-        copy.wait()
-
-    def join_a(q, _):
-        total = own[q, y, :, 0:wide]
-        for j in cols:
-            total += gota[j - 1, q].astype(F32)
-        acca[q] = total
-        return 0
-
-    lax.fori_loop(0, nz, join_a, 0)
-    for k in rings:
-        pz = lax.rem(z + k, nz)
-        second_a.append(remote(acca.at[pz], gota2.at[k - 1], s_a2.at[k - 1], r_a2.at[k - 1], chip(0, 0, k, c)))
-    for copy in second_a:
-        copy.start()
-    for copy in first_b:
-        copy.wait()
-
-    def join_b(q, _):
-        total = own[z, q, :, wide:]
-        for k in rings:
-            total += gotb[k - 1, q].astype(F32)
-        accb[q] = total
-        return 0
-
-    lax.fori_loop(0, ny, join_b, 0)
-    for j in cols:
-        py = lax.rem(y + j, ny)
-        second_b.append(remote(accb.at[py], gotb2.at[j - 1], s_b2.at[j - 1], r_b2.at[j - 1], chip(0, j, 0, c)))
-    for copy in second_b:
-        copy.start()
+    second_rows(1)
+    finish_rows(0)
 
     def pass_on(first, n):
         part = enc_out.at[c, pl.ds(pl.multiple_of(first, piece), piece), :]
@@ -417,18 +460,7 @@
         source = lax.rem(x + nx - i, nx) * ny + lax.rem(y + ny - j, ny)
         handed.append(pass_on(source * piece, nz + 1 + n))
 
-    for copy in second_a:
-        copy.wait()
-    total = acca[z]
-    for k in rings:
-        total += gota2[k - 1]
-    slab_out[:, 0:wide] = total
-    for copy in second_b:
-        copy.wait()
-    total = accb[y]
-    for j in cols:
-        total += gotb2[j - 1]
-    slab_out[:, wide:] = total
+    finish_rows(1)
     for copy in handed:
         copy.wait()
 
@@ -441,8 +473,9 @@
     picks = shortlist.shape[1]
     plane = nx * ny
     depth = held // (ny * nz)
-    wide = 2 * width // 3
-    slim = width - wide
+    part = width // 2
+    wide = 2 * part // 3
+    slim = part - wide
     half = width // 2
     piece = half // (plane + nz)
     share = piece // nz
@@ -452,6 +485,7 @@
     i32 = lambda *shape: pltpu.VMEM(shape, I32)
     i16 = lambda *shape: pltpu.VMEM(shape, I16)
     dma = lambda n: [pltpu.SemaphoreType.DMA((n,))] * 2
+    two = lambda n: [pltpu.SemaphoreType.DMA((2, n))] * 2
     vmem = pl.BlockSpec(memory_space=pltpu.VMEM)
     slab_grad, enc_grad = pl.pallas_call(
         functools.partial(step_kernel, dims),
@@ -465,18 +499,18 @@
             b16(owners, cap, width), b16(owners, cap, width),
             b16(owners, 16, cap), b16(owners, 16, cap), i32(owners, 1, cap),
             i16(slot_count, docs), b16(slot_count, docs),
-            b16(owners, cap, width), b16(owners, cap, width),
+            b16(2, owners, cap, part), b16(2, owners, cap, part),
             f32(nz, ny, depth, width), b16(nz, ny, depth, width),
-            b16(ny - 1, nz, depth, wide), b16(nz - 1, ny, depth, slim),
-            f32(nz, depth, wide), f32(ny, depth, slim),
-            f32(nz - 1, depth, wide), f32(ny - 1, depth, slim),
+            b16(2, ny - 1, nz, depth, wide), b16(2, nz - 1, ny, depth, slim),
+            f32(2, nz, depth, wide), f32(2, ny, depth, slim),
+            f32(2, nz - 1, depth, wide), f32(2, ny - 1, depth, slim),
             b16(docs, width), f32(2, half, width), f32(half, width),
             b16(plane, piece, width), b16(nz, piece, width),
             b16(plane - 1, piece, width), b16(nz - 1, piece, width),
             f32(nz, share, width), f32(nz - 1, share, width), f32(nz, share, width),
             f32(nx, piece, width), f32(ny, piece, width),
-            pltpu.SemaphoreType.DMA((8,)), *dma(owners), *dma(owners), *dma(owners), *dma(owners),
-            *dma(ny - 1), *dma(nz - 1), *dma(nz - 1), *dma(ny - 1),
+            pltpu.SemaphoreType.DMA((8,)), *dma(owners), *dma(owners), *dma(owners), *two(owners),
+            *two(ny - 1), *two(nz - 1), *two(nz - 1), *two(ny - 1),
             pltpu.SemaphoreType.DMA, pltpu.SemaphoreType.DMA,
             *dma(plane - 1), *dma(nz - 1), *dma(nz - 1), *dma(nz - 1), *dma(nx - 1), *dma(ny - 1), *dma(plane - 1), *dma(nz - 1),
             *dma(plane + nz),

time: 88.9 us -> 85.8 us (0.965)
  the two profiles are of different devices: /device:TPU:1 before, /device:TPU:19 now
where the time goes in v9:
time: 85.8 us; the launch traced here: 85.7 us
  Pallas kernels  83 us (97%)
  local copies, waits for them, and re-layouts  2.03 us (2%)
    pallas_call x1, Pallas kernels, body(): pl.pallas_call(functools.partial(step_kernel, dims), out_shape=(jax.Shape...  83 us
    unnamed x2, local copies, waits for them, and re-layouts  2.03 us

profile of v9, /device:TPU:19, one launch (start us, length us, event | category | flops | bytes accessed | tf_op | source)
XLA Modules:
  0.0 85.7 jit_solution(10573064876214745263)
XLA Ops:
  0.6 83.0 %classifier_step.1 = (f32[16,768]{1,0:T(8,128)S(1)}, f32[2,384,768]{2,1,0:T(8,128)S(1)}) custom-call(bf16[1024,768]{1,0:T(8,128)(2,1)} %docs_in.1, bf16[768,768]{1,0:T(8,128)(2,1)} %weight_in.1, bf16[512,768]{1,0:T(8,128)(2,1)} %slab_in.1, bf16[512]{0:T(512)(128)(2,1)} %scale_in.1, s32[8,1,128]{2,1,0:T(1,128)} %bitcast.7, s32[32,1024]{1,0:T(8,128)} %bitcast.5, ...), custom_call_target="tpu_custom_call" | custom-call | flops 10000000000 | bytes 10000000 | tf_op jit(solution)/shard_map/classifier_step/pallas_call | solution.py:490
  83.7 0.6 copy.12
  84.3 1.4 %copy.13 = f32[768,768]{1,0:T(8,128)} copy(f32[768,768]{1,0:T(8,128)S(1)} %bitcast.4) | data formatting | bytes 4718592

commit v10 on v9

--- a/solution.py
+++ b/solution.py
@@ -28,8 +28,8 @@
 
 def step_kernel(
     dims, docs_in, weight_in, slab_in, scale_in, ids_in, slots_in, on_in, counts_in, slab_out, enc_out,
-    ids, counts, scale, docs, weight, slab, slots32, on32, slots, marks, emb, slope, push, onehot, srows, frows, sscale, fscale, gids, tally, dscore, grads, back,
-    own, ownb, gota, gotb, acca, accb, gota2, gotb2,
+    ids, counts, scale, docs, weight, slab, slots32, on32, slots, marks, emb, slope, push, onehot, srows, frows, sscale, fscale, gids, tally, dscore, grads0, grads1, back0, back1,
+    own, ownb, gota0, gota1, gotb0, gotb1, acca0, acca1, accb0, accb1, gota20, gota21, gotb20, gotb21,
     inner, enc, sib, accp, accq, gotp, gotq, shares, gots, done, allx, ally,
     s_in, s_id, r_id, s_f, r_f, s_c, r_c, s_g, r_g,
     s_a, r_a, s_b, r_b, s_a2, r_a2, s_b2, r_b2,
@@ -45,8 +45,10 @@
     pair = 2 * cap
     documents, width = docs.shape
     rows_held = slab.shape[0]
-    wide = gota.shape[-1]
-    depth = gota.shape[-2]
+    depth = own.shape[-2]
+    grads, back = (grads0, grads1), (back0, back1)
+    gota, gotb, acca, accb = (gota0, gota1), (gotb0, gotb1), (acca0, acca1), (accb0, accb1)
+    gota2, gotb2 = (gota20, gota21), (gotb20, gotb21)
     piece = accp.shape[1]
     share = shares.shape[1]
     half = enc.shape[1]
@@ -158,12 +160,12 @@
     lax.fori_loop(0, owners, serve, 0)
 
     parts = range(2)
-    part_width = width // 2
+    starts, widths = (0, grads0.shape[-1]), (grads0.shape[-1], grads1.shape[-1])
 
     def grad_copy(h, n):
         _, source = peer(n)
         return remote(
-            grads.at[h, source], back.at[h, owner], s_g.at[h, n], r_g.at[h, n], {"owner": source, "dp": group}
+            grads[h].at[source], back[h].at[owner], s_g.at[h, n], r_g.at[h, n], {"owner": source, "dp": group}
         )
 
     loads[3].wait()
@@ -212,7 +214,8 @@
         first, span = group_of(r)
         product = jnp.dot(dscore[span, :], emb[...], preferred_element_type=F32).astype(BF16)
         for h in parts:
-            grads[h, pl.ds(first, 2)] = product[:, h * part_width : (h + 1) * part_width].reshape(2, cap, part_width)
+            mine = product[:, starts[h] : starts[h] + widths[h]]
+            grads[h][pl.ds(first, 2)] = mine.reshape(2, cap, widths[h])
 
     def pulled(r):
         first, span = group_of(r)
@@ -244,7 +247,7 @@
 
     lax.fori_loop(0, far, work, 0)
     for h in parts:
-        back[h, owner] = grads[h, owner]
+        back[h][owner] = grads[h][owner]
     arrived(2 * far)
     arrived(2 * far + 1)
     score(far)
@@ -290,27 +293,27 @@
         grad_copy(1, n).start()
 
     def cols_a(h):
-        return pl.ds(h * part_width, wide)
+        return pl.ds(starts[h], gota[h].shape[-1])
 
     def cols_b(h):
-        return pl.ds(h * part_width + wide, part_width - wide)
+        return pl.ds(starts[h] + gota[h].shape[-1], gotb[h].shape[-1])
 
     first_a, first_b, second_a, second_b = [[], []], [[], []], [[], []], [[], []]
 
     def sum_rows(h):
         for n in range(1, owners):
             grad_copy(h, n).wait()
-        total = jnp.dot(onehot[...], back[h].reshape(owners * cap, part_width), preferred_element_type=F32)
-        here_cols = pl.ds(h * part_width, part_width)
-        own[:, :, :, here_cols] = total.reshape(nz, ny, depth, part_width)
-        ownb[:, :, :, here_cols] = total.astype(BF16).reshape(nz, ny, depth, part_width)
+        total = jnp.dot(onehot[...], back[h][...].reshape(owners * cap, widths[h]), preferred_element_type=F32)
+        here_cols = pl.ds(starts[h], widths[h])
+        own[:, :, :, here_cols] = total.reshape(nz, ny, depth, widths[h])
+        ownb[:, :, :, here_cols] = total.astype(BF16).reshape(nz, ny, depth, widths[h])
         for j in cols:
             py = lax.rem(y + j, ny)
-            first_a[h].append(remote(ownb.at[:, py, :, cols_a(h)], gota.at[h, j - 1], s_a.at[h, j - 1],
+            first_a[h].append(remote(ownb.at[:, py, :, cols_a(h)], gota[h].at[j - 1], s_a.at[h, j - 1],
                                      r_a.at[h, j - 1], chip(0, j, 0, c)))
         for k in rings:
             pz = lax.rem(z + k, nz)
-            first_b[h].append(remote(ownb.at[pz, :, :, cols_b(h)], gotb.at[h, k - 1], s_b.at[h, k - 1],
+            first_b[h].append(remote(ownb.at[pz, :, :, cols_b(h)], gotb[h].at[k - 1], s_b.at[h, k - 1],
                                      r_b.at[h, k - 1], chip(0, 0, k, c)))
         for copy in first_a[h] + first_b[h]:
             copy.start()
@@ -322,14 +325,14 @@
         def join_a(q, _):
             total = own[q, y, :, cols_a(h)]
             for j in cols:
-                total += gota[h, j - 1, q].astype(F32)
-            acca[h, q] = total
+                total += gota[h][j - 1, q].astype(F32)
+            acca[h][q] = total
             return 0
 
         lax.fori_loop(0, nz, join_a, 0)
         for k in rings:
             pz = lax.rem(z + k, nz)
-            second_a[h].append(remote(acca.at[h, pz], gota2.at[h, k - 1], s_a2.at[h, k - 1], r_a2.at[h, k - 1],
+            second_a[h].append(remote(acca[h].at[pz], gota2[h].at[k - 1], s_a2.at[h, k - 1], r_a2.at[h, k - 1],
                                       chip(0, 0, k, c)))
         for copy in second_a[h]:
             copy.start()
@@ -339,14 +342,14 @@
         def join_b(q, _):
             total = own[z, q, :, cols_b(h)]
             for k in rings:
-                total += gotb[h, k - 1, q].astype(F32)
-            accb[h, q] = total
+                total += gotb[h][k - 1, q].astype(F32)
+            accb[h][q] = total
             return 0
 
         lax.fori_loop(0, ny, join_b, 0)
         for j in cols:
             py = lax.rem(y + j, ny)
-            second_b[h].append(remote(accb.at[h, py], gotb2.at[h, j - 1], s_b2.at[h, j - 1], r_b2.at[h, j - 1],
+            second_b[h].append(remote(accb[h].at[py], gotb2[h].at[j - 1], s_b2.at[h, j - 1], r_b2.at[h, j - 1],
                                       chip(0, j, 0, c)))
         for copy in second_b[h]:
             copy.start()
@@ -354,15 +357,15 @@
     def finish_rows(h):
         for copy in second_a[h]:
             copy.wait()
-        total = acca[h, z]
+        total = acca[h][z]
         for k in rings:
-            total += gota2[h, k - 1]
+            total += gota2[h][k - 1]
         slab_out[:, cols_a(h)] = total
         for copy in second_b[h]:
             copy.wait()
-        total = accb[h, y]
+        total = accb[h][y]
         for j in cols:
-            total += gotb2[h, j - 1]
+            total += gotb2[h][j - 1]
         slab_out[:, cols_b(h)] = total
 
     sum_rows(0)
@@ -473,9 +476,7 @@
     picks = shortlist.shape[1]
     plane = nx * ny
     depth = held // (ny * nz)
-    part = width // 2
-    wide = 2 * part // 3
-    slim = part - wide
+    parts = (2 * width // 3, width // 3)
     half = width // 2
     piece = half // (plane + nz)
     share = piece // nz
@@ -499,11 +500,11 @@
             b16(owners, cap, width), b16(owners, cap, width),
             b16(owners, 16, cap), b16(owners, 16, cap), i32(owners, 1, cap),
             i16(slot_count, docs), b16(slot_count, docs),
-            b16(2, owners, cap, part), b16(2, owners, cap, part),
+            *(b16(owners, cap, p) for p in parts), *(b16(owners, cap, p) for p in parts),
             f32(nz, ny, depth, width), b16(nz, ny, depth, width),
-            b16(2, ny - 1, nz, depth, wide), b16(2, nz - 1, ny, depth, slim),
-            f32(2, nz, depth, wide), f32(2, ny, depth, slim),
-            f32(2, nz - 1, depth, wide), f32(2, ny - 1, depth, slim),
+            *(b16(ny - 1, nz, depth, p // 2) for p in parts), *(b16(nz - 1, ny, depth, p // 2) for p in parts),
+            *(f32(nz, depth, p // 2) for p in parts), *(f32(ny, depth, p // 2) for p in parts),
+            *(f32(nz - 1, depth, p // 2) for p in parts), *(f32(ny - 1, depth, p // 2) for p in parts),
             b16(docs, width), f32(2, half, width), f32(half, width),
             b16(plane, piece, width), b16(nz, piece, width),
             b16(plane - 1, piece, width), b16(nz - 1, piece, width),

time: 85.8 us -> 82.2 us (0.958)
  the two profiles are of different devices: /device:TPU:19 before, /device:TPU:1 now
where the time goes in v10:
time: 82.2 us
  Pallas kernels  79.5 us (97%)
  local copies, waits for them, and re-layouts  2.03 us (2%)
    pallas_call x1, Pallas kernels, body(): pl.pallas_call(functools.partial(step_kernel, dims), out_shape=(jax.Shape...  79.5 us
    unnamed x2, local copies, waits for them, and re-layouts  2.03 us

profile of v10, /device:TPU:1, one launch (start us, length us, event | category | flops | bytes accessed | tf_op | source)
XLA Modules:
  0.0 82.2 jit_solution(4471685736907159489)
XLA Ops:
  0.6 79.5 %classifier_step.1 = (f32[16,768]{1,0:T(8,128)S(1)}, f32[2,384,768]{2,1,0:T(8,128)S(1)}) custom-call(bf16[1024,768]{1,0:T(8,128)(2,1)} %docs_in.1, bf16[768,768]{1,0:T(8,128)(2,1)} %weight_in.1, bf16[512,768]{1,0:T(8,128)(2,1)} %slab_in.1, bf16[512]{0:T(512)(128)(2,1)} %scale_in.1, s32[8,1,128]{2,1,0:T(1,128)} %bitcast.7, s32[32,1024]{1,0:T(8,128)} %bitcast.5, ...), custom_call_target="tpu_custom_call" | custom-call | flops 10000000000 | bytes 10000000 | tf_op jit(solution)/shard_map/classifier_step/pallas_call | solution.py:491
  80.1 0.6 copy.12
  80.7 1.4 %copy.13 = f32[768,768]{1,0:T(8,128)} copy(f32[768,768]{1,0:T(8,128)S(1)} %bitcast.4) | data formatting | bytes 4718592

commit v11 on v10

--- a/solution.py
+++ b/solution.py
@@ -30,10 +30,10 @@
     dims, docs_in, weight_in, slab_in, scale_in, ids_in, slots_in, on_in, counts_in, slab_out, enc_out,
     ids, counts, scale, docs, weight, slab, slots32, on32, slots, marks, emb, slope, push, onehot, srows, frows, sscale, fscale, gids, tally, dscore, grads0, grads1, back0, back1,
     own, ownb, gota0, gota1, gotb0, gotb1, acca0, acca1, accb0, accb1, gota20, gota21, gotb20, gotb21,
-    inner, enc, sib, accp, accq, gotp, gotq, shares, gots, done, allx, ally,
+    inner, sinner, sdocs, enc, accp, accq, gotp, gotq, shares, gots, done, allx, ally,
     s_in, s_id, r_id, s_f, r_f, s_c, r_c, s_g, r_g,
     s_a, r_a, s_b, r_b, s_a2, r_a2, s_b2, r_b2,
-    s_sib, r_sib, s_p, r_p, s_q, r_q, s_p2, r_p2, s_ag, r_ag, s_x, r_x, s_y, r_y, s_p3, r_p3, s_q3, r_q3, s_e, r_e,
+    s_sib, r_sib, s_doc, r_doc, s_p, r_p, s_q, r_q, s_p2, r_p2, s_ag, r_ag, s_x, r_x, s_y, r_y, s_p3, r_p3, s_q3, r_q3, s_e, r_e,
 ):
     nx, ny, nz = dims
     owner, group = lax.axis_index("owner"), lax.axis_index("dp")
@@ -51,7 +51,7 @@
     gota2, gotb2 = (gota20, gota21), (gotb20, gotb21)
     piece = accp.shape[1]
     share = shares.shape[1]
-    half = enc.shape[1]
+    mid = enc.shape[1]
     cut = nx * ny * piece
     strip = min(128, documents)
     far = nx - 1
@@ -108,6 +108,8 @@
     gids[owner] = ids[owner]
 
     loads[0].wait()
+    mate = remote(docs, sdocs, s_doc, r_doc, chip(0, 0, 0, 1 - c))
+    mate.start()
     loads[1].wait()
     squashed = jnp.tanh(jnp.dot(docs[...], weight[...], preferred_element_type=F32))
     emb[...] = (docs[...].astype(F32) + squashed).astype(BF16)
@@ -255,26 +257,34 @@
     grad_copy(0, 2 * far).start()
     grad_copy(0, 2 * far + 1).start()
 
-    inner[...] = ((push[...] + pulled(far)) * slope[...]).astype(BF16)
-
-    def outer(which):
-        side = docs[:, pl.ds(pl.multiple_of(which * half, half), half)]
-        enc[which] = lax.dot_general(side, inner[...], (((0,), (0,)), ((), ())), preferred_element_type=F32)
-
-    outer(1 - c)
-    swap = remote(enc.at[1 - c], sib, s_sib, r_sib, chip(0, 0, 0, 1 - c))
+    def finish_inner(which):
+        first, span = group_of(far)
+        lanes = pl.ds(pl.multiple_of(which * mid, mid), mid)
+        rows = frows[pl.ds(first, 2), :, lanes].reshape(pair, mid)
+        last = lax.dot_general(dscore[span, :], rows, (((0,), (0,)), ((), ())), preferred_element_type=F32)
+        inner[which] = ((push[:, lanes] + last) * slope[:, lanes]).astype(BF16)
+
+    def outer(side, other):
+        return lax.dot_general(side[...], other, (((0,), (0,)), ((), ())), preferred_element_type=F32)
+
+    finish_inner(1 - c)
+    swap = remote(inner.at[1 - c], sinner, s_sib, r_sib, chip(0, 0, 0, 1 - c))
     swap.start()
-    outer(c)
+    finish_inner(c)
+    enc[...] = outer(docs, inner[c])
     swap.wait()
+    mate.wait()
+    enc[...] += outer(sdocs, sinner[...])
+
+    def summed(first):
+        return enc[pl.ds(pl.multiple_of(first, piece), piece), :]
 
     def join_p(q, _):
-        rows = pl.ds(pl.multiple_of(q * piece, piece), piece)
-        accp[q] = (enc[c, rows, :] + sib[rows, :]).astype(BF16)
+        accp[q] = summed(q * piece).astype(BF16)
         return 0
 
     def join_q(q, _):
-        rows = pl.ds(pl.multiple_of(cut + q * piece, piece), piece)
-        accq[q] = (enc[c, rows, :] + sib[rows, :]).astype(BF16)
+        accq[q] = summed(cut + q * piece).astype(BF16)
         return 0
 
     lax.fori_loop(0, nx * ny, join_p, 0)
@@ -372,8 +382,7 @@
 
     for copy in p1:
         copy.wait()
-    rows = pl.ds(pl.multiple_of(here * piece, piece), piece)
-    total = enc[c, rows, :] + sib[rows, :]
+    total = summed(here * piece)
     for n in range(len(plane)):
         total += gotp[n].astype(F32)
     for k in range(nz):
@@ -386,8 +395,7 @@
         copy.start()
     for copy in q1:
         copy.wait()
-    rows = pl.ds(pl.multiple_of(cut + z * piece, piece), piece)
-    total = enc[c, rows, :] + sib[rows, :]
+    total = summed(cut + z * piece)
     for k in rings:
         total += gotq[k - 1].astype(F32)
     allx[x] = total
@@ -425,10 +433,11 @@
     p3, q3 = [], []
     for copy in p2:
         copy.wait()
+    side = pl.ds(pl.multiple_of(c * mid, mid), mid)
     rows_p = pl.ds(pl.multiple_of(here * piece, piece), piece)
-    enc_out[c, rows_p, :] = jnp.concatenate([done[k] for k in range(nz)], axis=0)
+    enc_out[rows_p, side] = jnp.concatenate([done[k] for k in range(nz)], axis=0)
     for n, (i, j) in enumerate(plane):
-        part = enc_out.at[c, rows_p, :]
+        part = enc_out.at[rows_p, side]
         p3.append(remote(part, part, s_p3.at[n], r_p3.at[n], chip(i, j, 0, c)))
     for copy in p3:
         copy.start()
@@ -438,9 +447,9 @@
     for j in cols:
         total += ally[j]
     rows_q = pl.ds(pl.multiple_of(cut + z * piece, piece), piece)
-    enc_out[c, rows_q, :] = total
-    for k in rings:
-        part = enc_out.at[c, rows_q, :]
+    enc_out[rows_q, side] = total
+    for k in rings:
+        part = enc_out.at[rows_q, side]
         q3.append(remote(part, part, s_q3.at[k - 1], r_q3.at[k - 1], chip(0, 0, k, c)))
     for copy in q3:
         copy.start()
@@ -449,7 +458,7 @@
     finish_rows(0)
 
     def pass_on(first, n):
-        part = enc_out.at[c, pl.ds(pl.multiple_of(first, piece), piece), :]
+        part = enc_out.at[pl.ds(pl.multiple_of(first, piece), piece), side]
         copy = remote(part, part, s_e.at[n], r_e.at[n], chip(0, 0, 0, 1 - c))
         copy.start()
         return copy
@@ -477,8 +486,8 @@
     plane = nx * ny
     depth = held // (ny * nz)
     parts = (2 * width // 3, width // 3)
-    half = width // 2
-    piece = half // (plane + nz)
+    mid = width // 2
+    piece = width // (plane + nz)
     share = piece // nz
     slot_count = owners * cap
     f32 = lambda *shape: pltpu.VMEM(shape, F32)
@@ -490,7 +499,7 @@
     vmem = pl.BlockSpec(memory_space=pltpu.VMEM)
     slab_grad, enc_grad = pl.pallas_call(
         functools.partial(step_kernel, dims),
-        out_shape=(jax.ShapeDtypeStruct((depth, width), F32), jax.ShapeDtypeStruct((2, half, width), F32)),
+        out_shape=(jax.ShapeDtypeStruct((depth, width), F32), jax.ShapeDtypeStruct((width, width), F32)),
         in_specs=[pl.BlockSpec(memory_space=pltpu.HBM)] * 8,
         out_specs=[vmem] * 2,
         scratch_shapes=[
@@ -505,13 +514,14 @@
             *(b16(ny - 1, nz, depth, p // 2) for p in parts), *(b16(nz - 1, ny, depth, p // 2) for p in parts),
             *(f32(nz, depth, p // 2) for p in parts), *(f32(ny, depth, p // 2) for p in parts),
             *(f32(nz - 1, depth, p // 2) for p in parts), *(f32(ny - 1, depth, p // 2) for p in parts),
-            b16(docs, width), f32(2, half, width), f32(half, width),
-            b16(plane, piece, width), b16(nz, piece, width),
-            b16(plane - 1, piece, width), b16(nz - 1, piece, width),
-            f32(nz, share, width), f32(nz - 1, share, width), f32(nz, share, width),
-            f32(nx, piece, width), f32(ny, piece, width),
+            b16(2, docs, mid), b16(docs, mid), b16(docs, width), f32(width, mid),
+            b16(plane, piece, mid), b16(nz, piece, mid),
+            b16(plane - 1, piece, mid), b16(nz - 1, piece, mid),
+            f32(nz, share, mid), f32(nz - 1, share, mid), f32(nz, share, mid),
+            f32(nx, piece, mid), f32(ny, piece, mid),
             pltpu.SemaphoreType.DMA((8,)), *dma(owners), *dma(owners), *dma(owners), *two(owners),
             *two(ny - 1), *two(nz - 1), *two(nz - 1), *two(ny - 1),
+            pltpu.SemaphoreType.DMA, pltpu.SemaphoreType.DMA,
             pltpu.SemaphoreType.DMA, pltpu.SemaphoreType.DMA,
             *dma(plane - 1), *dma(nz - 1), *dma(nz - 1), *dma(nz - 1), *dma(nx - 1), *dma(ny - 1), *dma(plane - 1), *dma(nz - 1),
             *dma(plane + nz),
@@ -531,7 +541,7 @@
         positive.T,
         counts,
     )))
-    return slab_grad, enc_grad.reshape(width, width)
+    return slab_grad, enc_grad
 
 
 def solution(mesh):

time: 82.2 us -> 81.9 us (level)
  no operation moved by 1% of the time
where the time goes in v11:
time: 81.9 us; the launch traced here: 81.8 us
  Pallas kernels  79.1 us (97%)
  local copies, waits for them, and re-layouts  2.03 us (2%)
    pallas_call x1, Pallas kernels, body(): pl.pallas_call(functools.partial(step_kernel, dims), out_shape=(jax.Shape...  79.1 us
    unnamed x2, local copies, waits for them, and re-layouts  2.03 us

profile of v11, /device:TPU:1, one launch (start us, length us, event | category | flops | bytes accessed | tf_op | source)
XLA Modules:
  0.0 81.8 jit_solution(14144021659664791279)
XLA Ops:
  0.6 79.1 %classifier_step.1 = (f32[16,768]{1,0:T(8,128)S(1)}, f32[768,768]{1,0:T(8,128)S(1)}) custom-call(bf16[1024,768]{1,0:T(8,128)(2,1)} %docs_in.1, bf16[768,768]{1,0:T(8,128)(2,1)} %weight_in.1, bf16[512,768]{1,0:T(8,128)(2,1)} %slab_in.1, bf16[512]{0:T(512)(128)(2,1)} %scale_in.1, s32[8,1,128]{2,1,0:T(1,128)} %bitcast.5, s32[32,1024]{1,0:T(8,128)} %bitcast.3, ...), custom_call_target="tpu_custom_call" | custom-call | flops 10000000000 | bytes 10000000 | tf_op jit(solution)/shard_map/classifier_step/pallas_call | solution.py:500
  79.8 0.6 copy.12
  80.4 1.4 %copy.13 = f32[768,768]{1,0:T(8,128)} copy(f32[768,768]{1,0:T(8,128)S(1)} %get-tuple-element.5) | data formatting | bytes 4718592

commit v12 on v11

--- a/solution.py
+++ b/solution.py
@@ -253,9 +253,6 @@
     arrived(2 * far)
     arrived(2 * far + 1)
     score(far)
-    row_grads(far)
-    grad_copy(0, 2 * far).start()
-    grad_copy(0, 2 * far + 1).start()
 
     def finish_inner(which):
         first, span = group_of(far)
@@ -270,6 +267,9 @@
     finish_inner(1 - c)
     swap = remote(inner.at[1 - c], sinner, s_sib, r_sib, chip(0, 0, 0, 1 - c))
     swap.start()
+    row_grads(far)
+    grad_copy(0, 2 * far).start()
+    grad_copy(0, 2 * far + 1).start()
     finish_inner(c)
     enc[...] = outer(docs, inner[c])
     swap.wait()
@@ -380,6 +380,18 @@
 
     sum_rows(0)
 
+    q2 = []
+    for copy in q1:
+        copy.wait()
+    total = summed(cut + z * piece)
+    for k in rings:
+        total += gotq[k - 1].astype(F32)
+    allx[x] = total
+    for i in range(1, nx):
+        q2.append(remote(allx.at[x], allx.at[x], s_x.at[i - 1], r_x.at[i - 1], chip(i, 0, 0, c)))
+    for copy in q2:
+        copy.start()
+
     for copy in p1:
         copy.wait()
     total = summed(here * piece)
@@ -387,23 +399,12 @@
         total += gotp[n].astype(F32)
     for k in range(nz):
         shares[k] = total[k * share : (k + 1) * share, :]
-    p2, q2 = [], []
+    p2 = []
     for k in rings:
         pz = lax.rem(z + k, nz)
         p2.append(remote(shares.at[pz], gots.at[k - 1], s_p2.at[k - 1], r_p2.at[k - 1], chip(0, 0, k, c)))
     for copy in p2:
         copy.start()
-    for copy in q1:
-        copy.wait()
-    total = summed(cut + z * piece)
-    for k in rings:
-        total += gotq[k - 1].astype(F32)
-    allx[x] = total
-    for i in range(1, nx):
-        q2.append(remote(allx.at[x], allx.at[x], s_x.at[i - 1], r_x.at[i - 1], chip(i, 0, 0, c)))
-    for copy in q2:
-        copy.start()
-
     second_rows(0)
     for copy in p2:
         copy.wait()

time: 81.9 us -> 81.9 us (level)
  no operation moved by 1% of the time
where the time goes in v12:
time: 81.9 us; the launch traced here: 81.8 us
  Pallas kernels  79.2 us (97%)
  local copies, waits for them, and re-layouts  2.03 us (2%)
    pallas_call x1, Pallas kernels, body(): pl.pallas_call(functools.partial(step_kernel, dims), out_shape=(jax.Shape...  79.2 us
    unnamed x2, local copies, waits for them, and re-layouts  2.03 us

profile of v12, /device:TPU:1, one launch (start us, length us, event | category | flops | bytes accessed | tf_op | source)
XLA Modules:
  0.0 81.8 jit_solution(12113998637724340360)
XLA Ops:
  0.6 79.2 %classifier_step.1 = (f32[16,768]{1,0:T(8,128)S(1)}, f32[768,768]{1,0:T(8,128)S(1)}) custom-call(bf16[1024,768]{1,0:T(8,128)(2,1)} %docs_in.1, bf16[768,768]{1,0:T(8,128)(2,1)} %weight_in.1, bf16[512,768]{1,0:T(8,128)(2,1)} %slab_in.1, bf16[512]{0:T(512)(128)(2,1)} %scale_in.1, s32[8,1,128]{2,1,0:T(1,128)} %bitcast.5, s32[32,1024]{1,0:T(8,128)} %bitcast.3, ...), custom_call_target="tpu_custom_call" | custom-call | flops 10000000000 | bytes 10000000 | tf_op jit(solution)/shard_map/classifier_step/pallas_call | solution.py:501
  79.8 0.6 copy.12
  80.4 1.4 %copy.13 = f32[768,768]{1,0:T(8,128)} copy(f32[768,768]{1,0:T(8,128)S(1)} %get-tuple-element.5) | data formatting | bytes 4718592

commit v13 on v12

--- a/solution.py
+++ b/solution.py
@@ -405,7 +405,6 @@
         p2.append(remote(shares.at[pz], gots.at[k - 1], s_p2.at[k - 1], r_p2.at[k - 1], chip(0, 0, k, c)))
     for copy in p2:
         copy.start()
-    second_rows(0)
     for copy in p2:
         copy.wait()
     total = shares[z]
@@ -429,6 +428,7 @@
     for copy in q2:
         copy.start()
 
+    second_rows(0)
     sum_rows(1)
 
     p3, q3 = [], []

time: 81.9 us -> 84.9 us (1.037)
  Pallas kernels: 79.2 us -> 82.2 us
    pallas_call x1, Pallas kernels: 79.2 us -> 82.2 us  [body(): pl.pallas_call(functools.partial(step_kernel, dims), out_shape=(jax.Shape...]
where the time goes in v13:
time: 84.9 us
  Pallas kernels  82.2 us (97%)
  local copies, waits for them, and re-layouts  2.03 us (2%)
    pallas_call x1, Pallas kernels, body(): pl.pallas_call(functools.partial(step_kernel, dims), out_shape=(jax.Shape...  82.2 us
    unnamed x2, local copies, waits for them, and re-layouts  2.03 us

profile of v13, /device:TPU:1, one launch (start us, length us, event | category | flops | bytes accessed | tf_op | source)
XLA Modules:
  0.0 84.9 jit_solution(867765871618438352)
XLA Ops:
  0.6 82.2 %classifier_step.1 = (f32[16,768]{1,0:T(8,128)S(1)}, f32[768,768]{1,0:T(8,128)S(1)}) custom-call(bf16[1024,768]{1,0:T(8,128)(2,1)} %docs_in.1, bf16[768,768]{1,0:T(8,128)(2,1)} %weight_in.1, bf16[512,768]{1,0:T(8,128)(2,1)} %slab_in.1, bf16[512]{0:T(512)(128)(2,1)} %scale_in.1, s32[8,1,128]{2,1,0:T(1,128)} %bitcast.5, s32[32,1024]{1,0:T(8,128)} %bitcast.3, ...), custom_call_target="tpu_custom_call" | custom-call | flops 10000000000 | bytes 10000000 | tf_op jit(solution)/shard_map/classifier_step/pallas_call | solution.py:501
  82.8 0.6 copy.12
  83.5 1.4 %copy.13 = f32[768,768]{1,0:T(8,128)} copy(f32[768,768]{1,0:T(8,128)S(1)} %get-tuple-element.5) | data formatting | bytes 4718592
